TPU v7x, 128 devices: a whole 4x4x4 slice. The times are simulated.
128 devices in a mesh: sector: 4 (over y_hi, core), ops: 32 (over x, z, y_lo).
Axes of the slice: x: 4, y: 4 (y_hi: 2, y_lo: 2; y = y_hi * 2 + y_lo), z: 4, core: 2. Of those that a mesh axis runs over, the one named last changes fastest.
Arguments:
- wavefunction: bfloat16 [4, 1024, 1024], P('sector', 'ops'), may hold values from -6 to 6
- diag_scale: float32 [4, 1024, 1024], P('sector', 'ops'), may hold values from 1 to 8
- sector_dims: int32 [4], P('sector'), may hold values from 512 to 1024
- left_ops: bfloat16 [4, 64, 1024, 1024], P('sector', 'ops'), may hold values from -0.1875 to 0.1875
- right_ops: bfloat16 [4, 64, 1024, 1024], P('sector', 'ops'), may hold values from -0.1875 to 0.1875
- weight_index: int32 [4, 64], P('sector', 'ops'), may hold values from 0 to 15
- weight_table: float32 [16], replicated, may hold values from -1 to 1
Outputs:
- basis: bfloat16 [4, 1024, 1024], P('sector', 'ops')
- energy: float32 [4], P('sector')
- next_ops: float32 [1024, 1024], P('ops')
All inputs are finite; a program needn't handle non-finite values.
Results may differ from a plain program's by a relative error of at most 0.025.
Values may be sent and summed in bfloat16 or wider, within the bound.
No kernel may reach another device: no remote copies, remote signals or barrier semaphores. Data moves between devices by JAX's collectives and lax.ppermute only.
A program may use at most 128 MiB of HBM per device.

v0:
```python
import jax
import jax.numpy as jnp
from jax import lax
from jax.sharding import Mesh
from jax.sharding import PartitionSpec as P

KEEP = 1024
OPS = ("ops_0", "ops_1", "ops_2")


def in_blocks(x, dim, count):
    shape = x.shape
    tiles = x.reshape(*shape[:dim], count, shape[dim] // count, *shape[dim + 1 :])
    return jnp.moveaxis(tiles, dim, 0)


def sent_and_summed(x, axis, dim):
    tiles = in_blocks(x, dim, lax.axis_size(axis))
    arrived = lax.all_to_all(tiles, axis, split_axis=0, concat_axis=0, tiled=True)
    return arrived.astype(jnp.float32).sum(axis=0)


def from_everyone(x, axis):
    count = lax.axis_size(axis)
    return lax.all_to_all(jnp.broadcast_to(x[None], (count, *x.shape)), axis, 0, 0, tiled=True)


def over_copies(x, axis):
    return from_everyone(x, axis).sum(axis=0)


def together(arrays, axis):
    ravelled, at, gathered = (jnp.concatenate([a.reshape(-1) for a in arrays]), 0, [])
    so_far = over_copies(ravelled, axis)
    for a in arrays:
        gathered.append(so_far[at : at + a.size].reshape(a.shape))
        at += a.size
    return tuple(gathered)


def filled_up(lines, count):
    spare = -lines.shape[0] % count
    if not spare:
        return lines
    return jnp.concatenate([lines, jnp.zeros((spare, *lines.shape[1:]), lines.dtype)])


def joined_along(tiles, dim):
    shape = list(tiles.shape[1:])
    shape[dim] *= tiles.shape[0]
    return jnp.moveaxis(tiles, 0, dim).reshape(shape)


def gathered_by_axis(x, axes, dim):
    far, near = axes
    first = from_everyone(x, far)
    tiles = jnp.swapaxes(from_everyone(first, near), 0, 1)
    return joined_along(tiles.reshape(-1, *x.shape), dim)


def summed_on_arrival(x, axis, dim):
    tiles = in_blocks(x, dim, lax.axis_size(axis))
    arrived = lax.all_to_all(tiles, axis, split_axis=0, concat_axis=0, tiled=True)
    return arrived.sum(axis=0)


def sum_in_two_steps(x, axes, dim):
    far, near = axes
    own = summed_on_arrival(in_blocks(x, dim, lax.axis_size(far)), near, dim + 1)
    return jnp.sum(lax.all_to_all(own, far, 0, 0, tiled=True), axis=0)


def total_of(x, axes):
    lines = x.reshape(-1, x.shape[-1])
    padded = filled_up(lines, lax.axis_size(axes[0]) * lax.axis_size(axes[1]))
    whole = gathered_by_axis(sum_in_two_steps(padded, axes, 0), axes, 0)
    return lax.slice_in_dim(whole, 0, len(lines)).reshape(x.shape)


def taken_together(x, axis):
    everything = from_everyone(x, axis)
    return jnp.sum(everything.astype(jnp.float32), axis=0)


def shards(wavefunction, diag_scale, sector_dims, left_ops, right_ops, weight_index, weight_table):
    psi_local = wavefunction[0]
    rows_dev = psi_local.shape[0]
    order_k = psi_local.shape[1]
    pair_count = left_ops.shape[1]
    first_row = lax.axis_index(OPS) * rows_dev
    dim = sector_dims[0]
    col_live = jnp.arange(order_k) < dim
    row_live = first_row + jnp.arange(rows_dev) < dim
    psi_masked = jnp.where(
        row_live[:, None] & col_live[None, :], psi_local, jnp.zeros_like(psi_local)
    )
    whole_psi = lax.all_gather(psi_masked, OPS, axis=0, tiled=True)
    onehot = (weight_index[0][:, None] == jnp.arange(weight_table.shape[0])[None, :]).astype(
        jnp.float32
    )
    coef = jnp.sum(onehot * weight_table[None, :], axis=1)
    total = jnp.zeros((rows_dev * lax.axis_size(OPS), order_k), jnp.float32)
    for sigma_pair in range(pair_count):
        left_rows = left_ops[0, sigma_pair]
        applied = jnp.dot(left_rows, whole_psi, preferred_element_type=jnp.float32).astype(
            jnp.bfloat16
        )
        term = lax.dot_general(
            applied,
            right_ops[0, sigma_pair],
            (((1,), (1,)), ((), ())),
            preferred_element_type=jnp.float32,
        )
        total = total + coef[sigma_pair] * term
    live_rows = jnp.arange(rows_dev * lax.axis_size(OPS)) < dim
    sigma = sent_and_summed(
        jnp.where(live_rows[:, None] & col_live[None, :], total, jnp.float32(0.0)).astype(
            jnp.bfloat16
        ),
        OPS,
        0,
    )
    psi_f = psi_masked.astype(jnp.float32)
    numer, denom = together((jnp.sum(psi_f * sigma), jnp.sum(psi_f * psi_f)), OPS)
    energy = numer / denom
    update = psi_f + (sigma - energy * psi_f) / diag_scale[0]
    gram = (
        total_of(
            jnp.dot(update.T, update, precision=lax.Precision.HIGHEST),
            ("ops_0", ("ops_1", "ops_2")),
        )
        / order_k
    )
    gram = gram + 0.001 * jnp.eye(KEEP, dtype=jnp.float32)
    factor = jnp.linalg.cholesky(gram)
    basis_local = jax.scipy.linalg.solve_triangular(factor, update.T, lower=True).T.astype(
        jnp.bfloat16
    )
    basis_full = lax.all_gather(basis_local, OPS, axis=0, tiled=True)
    summed = jnp.zeros((KEEP, KEEP), jnp.float32)
    for pair in range(pair_count):
        moved = jnp.dot(left_ops[0, pair], basis_full, preferred_element_type=jnp.float32).astype(
            jnp.bfloat16
        )
        rotated = jnp.dot(basis_full.T, moved, preferred_element_type=jnp.float32) / order_k
        summed = summed + coef[pair] * rotated
    owned = sent_and_summed(summed.astype(jnp.bfloat16), OPS, 0)
    next_rows = taken_together(owned.astype(jnp.bfloat16), "sector").astype(jnp.float32)
    return (basis_local[None], jnp.reshape(energy, (1,)), next_rows)


def solution(mesh):
    split = Mesh(
        mesh.devices.reshape(mesh.shape["sector"], 4, 4, 2), ("sector", "ops_0", "ops_1", "ops_2")
    )
    in_specs = (
        P("sector", OPS, None),
        P("sector", OPS, None),
        P("sector"),
        P("sector", OPS, None, None),
        P("sector", OPS, None, None),
        P("sector", OPS),
        P(),
    )
    out_specs = (P("sector", OPS, None), P("sector"), P(OPS, None))
    return jax.shard_map(
        shards, mesh=split, in_specs=in_specs, out_specs=out_specs, check_vma=False
    )
```

profile of v0, /device:TPU:1, one launch (start us, length us, event | category | flops | bytes accessed | tf_op | source)
XLA Modules:
  0.0 898.9 jit_solution(17486737315408500519)
XLA Ops:
  10.9 135.1 %all-gather.3.cloned.1.call-done = bf16[1024,1024]{1,0:T(8,128)(2,1)} async-done(((bf16[32,1024]{1,0:T(8,128)(2,1)}), bf16[1024,1024]{1,0:T(8,128)(2,1)}) %all-gather.3.cloned.1.call-update) | async-done | bytes 2097168 | tf_op jit(solution)/shard_map/all_gather | solution.py:97
  146.1 9.5 %fusion.6 = f32[1024,1024]{0,1:T(8,128)} fusion(bf16[1,2,1024,1024]{3,2,1,0:T(8,128)(2,1)} %param.11, bf16[1024,1024]{1,0:T(8,128)(2,1)} %all-gather.3.cloned.1.call-done, bf16[1,2,1024,1024]{3,2,1,0:T(8,128)(2,1)} %param.10), kind=kOutput, calls=%fused_computation.18 | convolution fusion | flops 4296015872 | bytes 10485760 | tf_op jit(solution)/shard_map/dot_general | solution.py:108
  155.5 10.9 %select_convert_fusion = bf16[1024,1024]{0,1:T(8,128)(2,1)} fusion(f32[1024,1024]{0,1:T(8,128)} %fusion.6, bf16[1,2,1024,1024]{3,2,1,0:T(8,128)(2,1)} %param.11, f32[]{:T(128)} %bitcast.6, f32[]{:T(128)} %bitcast.3, pred[1024]{0:T(1024)(128)(4,1)S(1)} %iota_compare_fusion.4, bf16[1024,1024]{1,0:T(8,128)(2,1)S(1)} %copy-done.4, ...), kind=kOutput, calls=%fused_computation.10 | convolution fusion | flops 4302307328 | bytes 12585984 | tf_op jit(solution)/shard_map/dot_general | solution.py:108
  166.4 2.9 copy.102
  169.3 24.7 %all_to_all.41 = bf16[32,32,1024]{2,1,0:T(8,128)(2,1)S(1)} all-to-all(bf16[32,32,1024]{2,1,0:T(8,128)(2,1)S(1)} %bitcast.181), channel_id=1, replica_groups=mesh['sector'=4,'ops_0'=4,'ops_1'=4,'ops_2'=2] {'ops_0','ops_1','ops_2'}, dimensions={0} | all-to-all | bytes 4194304 | tf_op jit(solution)/shard_map/all_to_all | solution.py:19
  196.4 12.5 %all_to_all.42 = f32[32,1,2]{2,1,0:T(1,128)S(1)} all-to-all(f32[32,1,2]{2,1,0:T(1,128)S(1)} %broadcast_in_dim.21), channel_id=1, replica_groups=mesh['sector'=4,'ops_0'=4,'ops_1'=4,'ops_2'=2] {'ops_0','ops_1','ops_2'}, dimensions={0} | all-to-all | bytes 512 | tf_op jit(solution)/shard_map/all_to_all | solution.py:25
  211.2 3.5 convolution_bitcast_fusion
  215.3 30.6 %all_to_all.43 = f32[8,4,32,1024]{3,2,1,0:T(8,128)} all-to-all(f32[8,4,32,1024]{3,2,1,0:T(8,128)S(1)} %copy.105), channel_id=1, replica_groups=mesh['sector'=4,'ops_0'=4,'ops_1'=4,'ops_2'=2] {'ops_1','ops_2'}, dimensions={0} | all-to-all | bytes 8388608 | tf_op jit(solution)/shard_map/all_to_all | solution.py:63
  245.9 2.6 reduce_sum.92
  248.5 12.1 %all_to_all.44 = f32[4,32,1024]{2,1,0:T(8,128)S(1)} all-to-all(f32[4,32,1024]{2,1,0:T(8,128)S(1)} %reduce_sum.92), channel_id=1, replica_groups=mesh['sector'=4,'ops_0'=4,'ops_1'=4,'ops_2'=2] {'ops_0'}, dimensions={0} | all-to-all | bytes 1048576 | tf_op jit(solution)/shard_map/all_to_all | solution.py:70
  260.7 9.3 %all_to_all.45 = f32[4,32,1024]{2,1,0:T(8,128)S(1)} all-to-all(f32[4,32,1024]{2,1,0:T(8,128)S(1)} %broadcast_in_dim.24), channel_id=1, replica_groups=mesh['sector'=4,'ops_0'=4,'ops_1'=4,'ops_2'=2] {'ops_0'}, dimensions={0} | all-to-all | bytes 1048576 | tf_op jit(solution)/shard_map/all_to_all | solution.py:25
  270.0 2.5 broadcast_in_dim.25
  272.5 4.5 all-to-all-start.5
  277.2 27.2 %all-to-all-done.5 = f32[8,4,32,1024]{3,2,1,0:T(8,128)} async-done(((f32[8,4,32,1024]{3,2,1,0:T(8,128)}), f32[8,4,32,1024]{3,2,1,0:T(8,128)}, u32[]{:S(2)}, u32[]{:S(2)}) %all-to-all-start.5) | async-done | bytes 4194336 | tf_op jit(solution)/shard_map/all_to_all | solution.py:25
  304.3 5.0 copy_multiply_fusion
  309.3 5.3 copy.107
  314.7 4.8 select_add_fusion
  319.5 5.7 copy.108
  325.3 4.5 fusion
  331.6 11.7 %cholesky.222 = f32[128,128]{1,0:T(8,128)S(1)} custom-call(f32[128,128]{1,0:T(8,128)S(1)} %cholesky.577), custom_call_target="Cholesky" | custom-call | tf_op jit(solution)/shard_map/jit(cholesky)/cholesky | solution.py:135
  343.5 9.8 %custom-call.63 = f32[1,128,128]{1,2,0:T(8,128)S(1)} custom-call(f32[1,128,128]{2,1,0:T(8,128)S(1)} %get-tuple-element.56), custom_call_target="InvertDiagBlocksLowerTriangular" | custom-call | tf_op jit(solution)/shard_map/jit(cholesky)/cholesky | solution.py:135
  356.6 11.7 %cholesky.243 = f32[128,128]{1,0:T(8,128)S(1)} custom-call(f32[128,128]{1,0:T(8,128)S(1)} %cholesky.581), custom_call_target="Cholesky" | custom-call | tf_op jit(solution)/shard_map/jit(cholesky)/cholesky | solution.py:135
  368.6 2.5 cholesky.254
  371.1 9.8 %custom-call.64 = f32[1,128,128]{1,2,0:T(8,128)S(1)} custom-call(f32[1,128,128]{2,1,0:T(8,128)S(1)} %get-tuple-element.54), custom_call_target="InvertDiagBlocksLowerTriangular" | custom-call | tf_op jit(solution)/shard_map/jit(cholesky)/cholesky | solution.py:135
  383.7 2.7 convolution_subtract_fusion.1
  386.4 11.7 %cholesky.466 = f32[128,128]{1,0:T(8,128)S(1)} custom-call(f32[128,128]{1,0:T(8,128)S(1)} %cholesky.586), custom_call_target="Cholesky" | custom-call | tf_op jit(solution)/shard_map/jit(cholesky)/cholesky | solution.py:135
  398.9 9.8 %custom-call.65 = f32[1,128,128]{1,2,0:T(8,128)S(1)} custom-call(f32[1,128,128]{2,1,0:T(8,128)S(1)} %get-tuple-element.52), custom_call_target="InvertDiagBlocksLowerTriangular" | custom-call | tf_op jit(solution)/shard_map/jit(cholesky)/cholesky | solution.py:135
  410.0 3.3 convolution_subtract_fusion.2
  413.4 11.7 %cholesky.485 = f32[128,128]{1,0:T(8,128)S(1)} custom-call(f32[128,128]{1,0:T(8,128)S(1)} %cholesky.591), custom_call_target="Cholesky" | custom-call | tf_op jit(solution)/shard_map/jit(cholesky)/cholesky | solution.py:135
  425.9 9.8 %custom-call.66 = f32[1,128,128]{1,2,0:T(8,128)S(1)} custom-call(f32[1,128,128]{2,1,0:T(8,128)S(1)} %get-tuple-element.50), custom_call_target="InvertDiagBlocksLowerTriangular" | custom-call | tf_op jit(solution)/shard_map/jit(cholesky)/cholesky | solution.py:135
  436.8 3.1 convolution_subtract_fusion.3
  440.0 12.1 %cholesky.504 = f32[128,128]{1,0:T(8,128)S(1)} custom-call(f32[128,128]{1,0:T(8,128)S(1)} %cholesky.596), custom_call_target="Cholesky" | custom-call | tf_op jit(solution)/shard_map/jit(cholesky)/cholesky | solution.py:135
  452.9 9.8 %custom-call.67 = f32[1,128,128]{1,2,0:T(8,128)S(1)} custom-call(f32[1,128,128]{2,1,0:T(8,128)S(1)} %get-tuple-element.48), custom_call_target="InvertDiagBlocksLowerTriangular" | custom-call | tf_op jit(solution)/shard_map/jit(cholesky)/cholesky | solution.py:135
  463.8 3.1 convolution_subtract_fusion.4
  466.9 11.7 %cholesky.524 = f32[128,128]{1,0:T(8,128)S(1)} custom-call(f32[128,128]{1,0:T(8,128)S(1)} %cholesky.601), custom_call_target="Cholesky" | custom-call | tf_op jit(solution)/shard_map/jit(cholesky)/cholesky | solution.py:135
  479.4 9.8 %custom-call.68 = f32[1,128,128]{1,2,0:T(8,128)S(1)} custom-call(f32[1,128,128]{2,1,0:T(8,128)S(1)} %get-tuple-element.46), custom_call_target="InvertDiagBlocksLowerTriangular" | custom-call | tf_op jit(solution)/shard_map/jit(cholesky)/cholesky | solution.py:135
  490.2 2.8 convolution_subtract_fusion.5
  493.0 11.7 %cholesky.544 = f32[128,128]{1,0:T(8,128)S(1)} custom-call(f32[128,128]{1,0:T(8,128)S(1)} %cholesky.606), custom_call_target="Cholesky" | custom-call | tf_op jit(solution)/shard_map/jit(cholesky)/cholesky | solution.py:135
  505.5 9.8 %custom-call.69 = f32[1,128,128]{1,2,0:T(8,128)S(1)} custom-call(f32[1,128,128]{2,1,0:T(8,128)S(1)} %get-tuple-element.44), custom_call_target="InvertDiagBlocksLowerTriangular" | custom-call | tf_op jit(solution)/shard_map/jit(cholesky)/cholesky | solution.py:135
  518.4 11.7 %cholesky.562 = f32[128,128]{1,0:T(8,128)S(1)} custom-call(f32[128,128]{1,0:T(8,128)S(1)} %convolution_subtract_fusion.6), custom_call_target="Cholesky" | custom-call | tf_op jit(solution)/shard_map/jit(cholesky)/cholesky | solution.py:135
  540.6 4.8 select_select_fusion
  545.4 23.7 %while.1 = (s32[]{:T(128)}, f32[1024,1024]{0,1:T(8,128)}, s32[8,2]{0,1:T(2,128)S(1)}, f32[8,128,128]{2,1,0:T(8,128)S(1)}, s32[]{:T(128)}) while((s32[]{:T(128)}, f32[1024,1024]{0,1:T(8,128)}, s32[8,2]{0,1:T(2,128)S(1)}, f32[8,128,128]{2,1,0:T(8,128)S(1)}, s32[]{:T(128)}) %tuple.57), condition=%wide.while_cond, body=%wide.while_body.sunk | while | flops 2 | bytes 393329 | solution.py:136
  569.2 78.8 %custom-call.70 = f32[8,128,128]{1,2,0:T(8,128)S(1)} custom-call(f32[8,128,128]{2,1,0:T(8,128)S(1)} %get-tuple-element.10), custom_call_target="InvertDiagBlocksLowerTriangular" | custom-call | tf_op jit(solution)/shard_map/jit(_solve_triangular)/triangular_solve | solution.py:136
  660.0 153.5 %all-gather.5.cloned.1.call-done = bf16[1024,1024]{1,0:T(8,128)(2,1)} async-done(((bf16[32,1024]{1,0:T(8,128)(2,1)}), bf16[1024,1024]{1,0:T(8,128)(2,1)}) %all-gather.5.cloned.1.call-update) | async-done | bytes 2097168 | tf_op jit(solution)/shard_map/all_gather | solution.py:139
  813.5 9.5 %fusion.13 = f32[1024,1024]{1,0:T(8,128)} fusion(bf16[1024,1024]{1,0:T(8,128)(2,1)} %all-gather.5.cloned.1.call-done, bf16[1,2,1024,1024]{3,2,1,0:T(8,128)(2,1)} %param.10), kind=kOutput, calls=%fused_computation.25 | convolution fusion | flops 4296015872 | bytes 10485760 | tf_op jit(solution)/shard_map/dot_general | solution.py:145
  822.9 8.7 add_convert_fusion
  831.7 24.7 %all_to_all.46 = bf16[32,32,1024]{2,1,0:T(8,128)(2,1)S(1)} all-to-all(bf16[32,32,1024]{2,1,0:T(8,128)(2,1)} %bitcast.183), channel_id=1, replica_groups=mesh['sector'=4,'ops_0'=4,'ops_1'=4,'ops_2'=2] {'ops_0','ops_1','ops_2'}, dimensions={0} | all-to-all | bytes 4194304 | tf_op jit(solution)/shard_map/all_to_all | solution.py:19
  856.8 33.1 %all_to_all.47 = bf16[4,32,1024]{2,1,0:T(8,128)(2,1)S(1)} all-to-all(bf16[4,32,1024]{2,1,0:T(8,128)(2,1)S(1)} %broadcast_in_dim.27), channel_id=1, replica_groups=mesh['sector'=4,'ops_0'=4,'ops_1'=4,'ops_2'=2] {'sector'}, dimensions={0} | all-to-all | bytes 524288 | tf_op jit(solution)/shard_map/all_to_all | solution.py:25
  (148 shorter events, 67.6 us)
Async XLA Ops:
  7.2 138.9 %all-gather.3.cloned.1.call-start = ((), (), s32[]{:S(2)}) async-start(), calls=%async_computation.8 | async-start | bytes 2162688 | tf_op jit(solution)/shard_map/all_gather | solution.py:97
  146.1 9.5 %copy-start.4 = (bf16[1024,1024]{1,0:T(8,128)(2,1)S(1)}, bf16[1024,1024]{1,0:T(8,128)(2,1)}, u32[]{:S(2)}) copy-start(bf16[1024,1024]{1,0:T(8,128)(2,1)} %all-gather.3.cloned.1.call-done) | copy-start | bytes 6291460
  169.3 25.1 %copy-start.1 = (bf16[1,32,1024]{2,1,0:T(8,128)(2,1)S(1)}, bf16[1,32,1024]{2,1,0:T(8,128)(2,1)}, u32[]{:S(2)}) copy-start(bf16[1,32,1024]{2,1,0:T(8,128)(2,1)} %param.7) | copy-start | bytes 196612
  169.3 41.6 %copy-start.2 = (f32[1,32,1024]{2,1,0:T(8,128)S(1)}, f32[1,32,1024]{2,1,0:T(8,128)}, u32[]{:S(2)}) copy-start(f32[1,32,1024]{2,1,0:T(8,128)} %param.8) | copy-start | bytes 393220
  272.5 31.8 %all-to-all-start.5 = ((f32[8,4,32,1024]{3,2,1,0:T(8,128)}), f32[8,4,32,1024]{3,2,1,0:T(8,128)}, u32[]{:S(2)}, u32[]{:S(2)}) async-start(f32[8,4,32,1024]{3,2,1,0:T(8,128)} %broadcast_in_dim.25), calls=%async_computation.5 | async-start | bytes 8388608 | tf_op jit(solution)/shard_map/all_to_all | solution.py:25
  277.1 536.4 %all-gather.5.cloned.1.call-start = ((), (), s32[]{:S(2)}) async-start(), calls=%async_computation.9 | async-start | bytes 2162688 | tf_op jit(solution)/shard_map/all_gather | solution.py:139
  329.7 1.9 copy-start
  658.1 0.6 copy-start.3
  813.5 9.5 %copy-start.5 = (bf16[1024,1024]{1,0:T(8,128)(2,1)S(1)}, bf16[1024,1024]{1,0:T(8,128)(2,1)}, u32[]{:S(2)}) copy-start(bf16[1024,1024]{1,0:T(8,128)(2,1)} %all-gather.5.cloned.1.call-done) | copy-start | bytes 6291460
Sparse Core Ops, SparseCore 0:
  10.2 135.7 all-gather.2
  658.9 154.5 all-gather.4
where the time goes:
time: 908 us; the launch traced here: 899 us
  waiting for transfers between devices  316 us (35%)
  other arithmetic  274 us (30%)
  blocking collectives  147 us (16%)
  matrix products  78.9 us (9%)
  local copies, waits for them, and re-layouts  53.5 us (6%)
  between operations  24.4 us (3%)
    another operation x30, other arithmetic, shards(): factor = jnp.linalg.cholesky(gram)  168 us
    all_gather x1, waiting for transfers between devices, shards(): basis_full = lax.all_gather(basis_local, OPS, axis=0, tiled=True)  153 us
    all_gather x1, waiting for transfers between devices, shards(): whole_psi = lax.all_gather(psi_masked, OPS, axis=0, tiled=True)  135 us
    another operation x3, other arithmetic, shards(): jax.scipy.linalg.solve_triangular(factor, update.T, lower=True)  83.6 us
    all_to_all x3, blocking collectives, from_everyone(): lax.all_to_all(jnp.broadcast_to(x[None], (count, *x.shape)), axis, 0, 0,...  54.9 us
    all_to_all x2, blocking collectives, sent_and_summed(): lax.all_to_all(tiles, axis, split_axis=0, concat_axis=0, tiled=True)  49.4 us
    all_to_all x1, blocking collectives, summed_on_arrival(): lax.all_to_all(tiles, axis, split_axis=0, concat_axis=0, tiled=True)  30.6 us
    all_to_all x1, waiting for transfers between devices, from_everyone(): lax.all_to_all(jnp.broadcast_to(x[None], (count, *x.shape)), axis, 0, 0,...  27.2 us
  transfers between devices with their start and end apart: 3, of which 3 were waited for; matrix products, arithmetic and copies ran while one was open for 0% of the time, Pallas kernels for 0%

commit v1 on v0

v1 whole, which is shorter than its diff:
```python
import jax
import jax.numpy as jnp
from jax import lax
from jax.sharding import Mesh
from jax.sharding import PartitionSpec as P

OPS = ("ops_0", "ops_1", "ops_2")


def from_everyone(x, axis):
    count = lax.axis_size(axis)
    return lax.all_to_all(jnp.broadcast_to(x[None], (count, *x.shape)), axis, 0, 0, tiled=True)


def shards(wavefunction, diag_scale, sector_dims, left_ops, right_ops, weight_index, weight_table):
    psi_local = wavefunction[0]
    rows_dev, order_k = psi_local.shape
    owners = lax.axis_size(OPS)
    me = lax.axis_index(OPS)
    dim = sector_dims[0]
    live = jnp.arange(order_k) < dim
    row_live = me * rows_dev + jnp.arange(rows_dev) < dim
    psi_masked = jnp.where(row_live[:, None] & live[None, :], psi_local, jnp.bfloat16(0))
    psi = from_everyone(psi_masked, OPS).reshape(order_k, order_k)
    onehot = weight_index[0][:, None] == jnp.arange(weight_table.shape[0])[None, :]
    coef = jnp.sum(jnp.where(onehot, weight_table[None, :], jnp.float32(0)), axis=1)
    total = jnp.zeros((order_k, order_k), jnp.float32)
    for p in range(left_ops.shape[1]):
        applied = jnp.dot(left_ops[0, p], psi, preferred_element_type=jnp.float32)
        term = lax.dot_general(
            applied.astype(jnp.bfloat16),
            right_ops[0, p],
            (((1,), (1,)), ((), ())),
            preferred_element_type=jnp.float32,
        )
        total = total + coef[p] * term
    total = jnp.where(live[:, None] & live[None, :], total, jnp.float32(0))
    psi_f = psi.astype(jnp.float32)
    numer_part = jnp.sum(psi_f * total)
    denom = jnp.sum(psi_f * psi_f)
    arrived = lax.all_to_all(
        total.astype(jnp.bfloat16).reshape(owners, rows_dev, order_k), OPS, 0, 0, tiled=True
    )
    numer = jnp.sum(from_everyone(numer_part.reshape(1, 1), OPS))
    sigma = jnp.sum(arrived.astype(jnp.float32), axis=0)
    energy = numer / denom
    mine = psi_masked.astype(jnp.float32)
    update = mine + (sigma - energy * mine) / diag_scale[0]
    x = from_everyone(update.astype(jnp.bfloat16), OPS).reshape(order_k, order_k)
    gram = lax.dot_general(x, x, (((0,), (0,)), ((), ())), preferred_element_type=jnp.float32)
    gram = gram / order_k + 0.001 * jnp.eye(order_k, dtype=jnp.float32)
    factor = jnp.linalg.cholesky(gram)
    basis = jax.scipy.linalg.solve_triangular(factor, x.astype(jnp.float32).T, lower=True).T
    basis = basis.astype(jnp.bfloat16)
    mixed = coef[0] * left_ops[0, 0].astype(jnp.float32)
    for p in range(1, left_ops.shape[1]):
        mixed = mixed + coef[p] * left_ops[0, p].astype(jnp.float32)
    moved = jnp.dot(mixed.astype(jnp.bfloat16), basis, preferred_element_type=jnp.float32)
    summed = lax.dot_general(
        basis,
        moved.astype(jnp.bfloat16),
        (((0,), (0,)), ((), ())),
        preferred_element_type=jnp.float32,
    )
    summed = (summed / order_k).astype(jnp.bfloat16).reshape(owners, rows_dev, order_k)
    owned = jnp.sum(
        lax.all_to_all(summed, OPS, 0, 0, tiled=True).astype(jnp.float32), axis=0
    )
    next_rows = jnp.sum(
        from_everyone(owned.astype(jnp.bfloat16), "sector").astype(jnp.float32), axis=0
    )
    basis_local = lax.dynamic_slice_in_dim(basis, me * rows_dev, rows_dev, axis=0)
    return (basis_local[None], jnp.reshape(energy, (1,)), next_rows)


def solution(mesh):
    split = Mesh(
        mesh.devices.reshape(mesh.shape["sector"], 4, 4, 2), ("sector", "ops_0", "ops_1", "ops_2")
    )
    in_specs = (
        P("sector", OPS, None),
        P("sector", OPS, None),
        P("sector"),
        P("sector", OPS, None, None),
        P("sector", OPS, None, None),
        P("sector", OPS),
        P(),
    )
    out_specs = (P("sector", OPS, None), P("sector"), P(OPS, None))
    return jax.shard_map(
        shards, mesh=split, in_specs=in_specs, out_specs=out_specs, check_vma=False
    )
```

time: 908 us -> 580 us (0.64)
  waiting for transfers between devices: 316 us -> 82 us
  blocking collectives: 147 us -> 49.1 us
  starting transfers between devices: 4.62 us -> 29.7 us
  between operations: 24.4 us -> 9.52 us
    all_gather x2 -> x0, waiting for transfers between devices: 289 us -> none  [the longest x1 153 us: shards(): basis_full = lax.all_gather(basis_local, OPS, axis=0, tiled=True)]
    all_to_all x4 -> x1, blocking collectives: 92.1 us -> 34.8 us  [shards(): lax.all_to_all(summed, OPS, 0, 0, tiled=True).astype(jnp.float32)]
    all_to_all x3 -> x1, blocking collectives: 54.9 us -> 14.3 us  [from_everyone(): lax.all_to_all(jnp.broadcast_to(x[None], (count, *x.shape)), axis, 0, 0,...]
    all_to_all x1 -> x3, waiting for transfers between devices: 27.2 us -> 59.4 us  [from_everyone(): lax.all_to_all(jnp.broadcast_to(x[None], (count, *x.shape)), axis, 0, 0,...]
    all_to_all x0 -> x1, waiting for transfers between devices: none -> 22.6 us  [shards(): lax.all_to_all(total.astype(jnp.bfloat16).reshape(owners, rows_dev, order...]
    all_to_all x1 -> x3, starting transfers between devices: 4.54 us -> 24.8 us  [from_everyone(): lax.all_to_all(jnp.broadcast_to(x[None], (count, *x.shape)), axis, 0, 0,...]
    another operation x15, matrix products: 9.91 us -> 27.1 us  [shards(): jax.scipy.linalg.solve_triangular(factor, x.astype(jnp.float32).T, lower=...]
    dot_general x5 -> x4, matrix products: 42 us -> 32.7 us  [the longest x2 19.7 us: shards(): lax.dot_general(applied.astype(jnp.bfloat16), right_ops[0, p], (((1,), (1...]
  transfers between devices with their start and end apart: 3 -> 4, of which waited for: 3 -> 4; matrix products, arithmetic and copies ran while one was open for 0% -> 1% of each run, Pallas kernels for 0% -> 0%
where the time goes in v1:
time: 580 us; the launch traced here: 571 us
  other arithmetic  272 us (47%)
  matrix products  83 us (14%)
  waiting for transfers between devices  82 us (14%)
  blocking collectives  49.1 us (8%)
  local copies, waits for them, and re-layouts  45.3 us (8%)
  starting transfers between devices  29.7 us (5%)
  between operations  9.52 us (2%)
    another operation x30, other arithmetic, shards(): factor = jnp.linalg.cholesky(gram)  173 us
    another operation x3, other arithmetic, shards(): jax.scipy.linalg.solve_triangular(factor, x.astype(jnp.float32).T, lower=...  83.4 us
    all_to_all x3, waiting for transfers between devices, from_everyone(): lax.all_to_all(jnp.broadcast_to(x[None], (count, *x.shape)), axis, 0, 0,...  59.4 us
    all_to_all x1, blocking collectives, shards(): lax.all_to_all(summed, OPS, 0, 0, tiled=True).astype(jnp.float32)  34.8 us
    another operation x15, matrix products, shards(): jax.scipy.linalg.solve_triangular(factor, x.astype(jnp.float32).T, lower=...  27.1 us
    all_to_all x3, starting transfers between devices, from_everyone(): lax.all_to_all(jnp.broadcast_to(x[None], (count, *x.shape)), axis, 0, 0,...  24.8 us
    another operation x14, matrix products, shards(): factor = jnp.linalg.cholesky(gram)  23.1 us
    all_to_all x1, waiting for transfers between devices, shards(): lax.all_to_all(total.astype(jnp.bfloat16).reshape(owners, rows_dev, order...  22.6 us
  transfers between devices with their start and end apart: 4, of which 4 were waited for; matrix products, arithmetic and copies ran while one was open for 1% of the time, Pallas kernels for 0%

profile of v1, /device:TPU:1, one launch (start us, length us, event | category | flops | bytes accessed | tf_op | source)
XLA Modules:
  0.0 570.8 jit_solution(16083362479075370809)
XLA Ops:
  3.9 9.7 %all-to-all-start = ((bf16[32,32,1024]{2,1,0:T(8,128)(2,1)}), bf16[32,32,1024]{2,1,0:T(8,128)(2,1)S(1)}, u32[]{:S(2)}, u32[]{:S(2)}) async-start(bf16[32,32,1024]{2,1,0:T(8,128)(2,1)} %broadcast_in_dim.62), calls=%async_computation | async-start | bytes 4194304 | tf_op jit(solution)/shard_map/all_to_all | solution.py:12
  14.4 26.9 %all-to-all-done = bf16[32,32,1024]{2,1,0:T(8,128)(2,1)S(1)} async-done(((bf16[32,32,1024]{2,1,0:T(8,128)(2,1)}), bf16[32,32,1024]{2,1,0:T(8,128)(2,1)S(1)}, u32[]{:S(2)}, u32[]{:S(2)}) %all-to-all-start) | async-done | bytes 2097184 | tf_op jit(solution)/shard_map/all_to_all | solution.py:12
  41.3 8.7 %fusion.14 = f32[1024,1024]{1,0:T(8,128)} fusion(bf16[1,2,1024,1024]{3,2,1,0:T(8,128)(2,1)} %param.11, bf16[1024,1024]{1,0:T(8,128)(2,1)S(1)} %bitcast.180, bf16[1,2,1024,1024]{3,2,1,0:T(8,128)(2,1)} %param.10), kind=kOutput, calls=%fused_computation.28 | convolution fusion | flops 4296015872 | bytes 10485760 | tf_op jit(solution)/shard_map/dot_general | solution.py:30
  50.0 11.0 %fusion.106 = (bf16[1024,1024]{1,0:T(8,128)(2,1)}, f32[]{:T(128)}) fusion(bf16[32,32,1024]{2,1,0:T(8,128)(2,1)S(1)} %all-to-all-done, bf16[1,2,1024,1024]{3,2,1,0:T(8,128)(2,1)} %param.11, bf16[1024,1024]{1,0:T(8,128)(2,1)S(1)} %bitcast.181, bf16[1,2,1024,1024]{3,2,1,0:T(8,128)(2,1)} %param.10, f32[]{:T(128)} %bitcast.7, f32[1024,1024]{1,0:T(8,128)} %fusion.14, ...), kind=kOutput, calls=%fused_computation.203 | convolution fusion | flops 4305453056 | bytes 14683140 | tf_op jit(solution)/shard_map/dot_general | solution.py:30
  61.7 14.3 %all_to_all.30 = f32[32,1,1]{2,1,0:T(1,128)S(1)} all-to-all(f32[32,1,1]{2,1,0:T(1,128)S(1)} %broadcast_in_dim.64), channel_id=1, replica_groups=mesh['sector'=4,'ops_0'=4,'ops_1'=4,'ops_2'=2] {'ops_0','ops_1','ops_2'}, dimensions={0} | all-to-all | bytes 256 | tf_op jit(solution)/shard_map/all_to_all | solution.py:12
  76.1 4.9 all-to-all-start.1
  84.6 22.6 %all-to-all-done.1 = bf16[32,32,1024]{2,1,0:T(8,128)(2,1)} async-done(((bf16[32,32,1024]{2,1,0:T(8,128)(2,1)}), bf16[32,32,1024]{2,1,0:T(8,128)(2,1)}, u32[]{:S(2)}, u32[]{:S(2)}) %all-to-all-start.1) | async-done | bytes 2097184 | tf_op jit(solution)/shard_map/all_to_all | solution.py:41
  110.9 8.6 %all-to-all-start.3 = ((bf16[32,32,1024]{2,1,0:T(8,128)(2,1)}), bf16[32,32,1024]{2,1,0:T(8,128)(2,1)S(1)}, u32[]{:S(2)}, u32[]{:S(2)}) async-start(bf16[32,32,1024]{2,1,0:T(8,128)(2,1)} %broadcast_in_dim.66), calls=%async_computation.3 | async-start | bytes 4194304 | tf_op jit(solution)/shard_map/all_to_all | solution.py:12
  119.5 27.7 %all-to-all-done.3 = bf16[32,32,1024]{2,1,0:T(8,128)(2,1)S(1)} async-done(((bf16[32,32,1024]{2,1,0:T(8,128)(2,1)}), bf16[32,32,1024]{2,1,0:T(8,128)(2,1)S(1)}, u32[]{:S(2)}, u32[]{:S(2)}) %all-to-all-start.3) | async-done | bytes 2097184 | tf_op jit(solution)/shard_map/all_to_all | solution.py:12
  147.2 2.4 fusion.110
  151.5 2.4 fusion
  153.9 5.3 copy.15
  159.2 4.5 add_multiply_fusion
  165.7 11.7 %cholesky.222 = f32[128,128]{1,0:T(8,128)S(1)} custom-call(f32[128,128]{1,0:T(8,128)S(1)} %cholesky.577), custom_call_target="Cholesky" | custom-call | tf_op jit(solution)/shard_map/jit(cholesky)/cholesky | solution.py:52
  177.4 2.5 cholesky.254
  179.9 3.1 copy.16
  183.0 2.4 bitcast_convert_fusion
  185.4 9.8 %custom-call.63 = f32[1,128,128]{1,2,0:T(8,128)S(1)} custom-call(f32[1,128,128]{2,1,0:T(8,128)S(1)} %get-tuple-element.70), custom_call_target="InvertDiagBlocksLowerTriangular" | custom-call | tf_op jit(solution)/shard_map/jit(cholesky)/cholesky | solution.py:52
  195.2 2.3 constant_dynamic-update-slice_fusion.25
  199.1 11.7 %cholesky.243 = f32[128,128]{1,0:T(8,128)S(1)} custom-call(f32[128,128]{1,0:T(8,128)S(1)} %cholesky.581), custom_call_target="Cholesky" | custom-call | tf_op jit(solution)/shard_map/jit(cholesky)/cholesky | solution.py:52
  211.5 9.8 %custom-call.64 = f32[1,128,128]{1,2,0:T(8,128)S(1)} custom-call(f32[1,128,128]{2,1,0:T(8,128)S(1)} %get-tuple-element.67), custom_call_target="InvertDiagBlocksLowerTriangular" | custom-call | tf_op jit(solution)/shard_map/jit(cholesky)/cholesky | solution.py:52
  224.7 12.1 %cholesky.466 = f32[128,128]{1,0:T(8,128)S(1)} custom-call(f32[128,128]{1,0:T(8,128)S(1)} %cholesky.586), custom_call_target="Cholesky" | custom-call | tf_op jit(solution)/shard_map/jit(cholesky)/cholesky | solution.py:52
  238.1 9.8 %custom-call.65 = f32[1,128,128]{1,2,0:T(8,128)S(1)} custom-call(f32[1,128,128]{2,1,0:T(8,128)S(1)} %get-tuple-element.64), custom_call_target="InvertDiagBlocksLowerTriangular" | custom-call | tf_op jit(solution)/shard_map/jit(cholesky)/cholesky | solution.py:52
  249.1 2.3 convolution_subtract_fusion.7
  251.4 11.7 %cholesky.485 = f32[128,128]{1,0:T(8,128)S(1)} custom-call(f32[128,128]{1,0:T(8,128)S(1)} %cholesky.591), custom_call_target="Cholesky" | custom-call | tf_op jit(solution)/shard_map/jit(cholesky)/cholesky | solution.py:52
  264.5 10.0 %custom-call.66 = f32[1,128,128]{1,2,0:T(8,128)S(1)} custom-call(f32[1,128,128]{2,1,0:T(8,128)S(1)} %get-tuple-element.61), custom_call_target="InvertDiagBlocksLowerTriangular" | custom-call | tf_op jit(solution)/shard_map/jit(cholesky)/cholesky | solution.py:52
  275.5 2.4 convolution_subtract_fusion.8
  277.9 11.7 %cholesky.504 = f32[128,128]{1,0:T(8,128)S(1)} custom-call(f32[128,128]{1,0:T(8,128)S(1)} %cholesky.596), custom_call_target="Cholesky" | custom-call | tf_op jit(solution)/shard_map/jit(cholesky)/cholesky | solution.py:52
  291.0 9.8 %custom-call.67 = f32[1,128,128]{1,2,0:T(8,128)S(1)} custom-call(f32[1,128,128]{2,1,0:T(8,128)S(1)} %get-tuple-element.58), custom_call_target="InvertDiagBlocksLowerTriangular" | custom-call | tf_op jit(solution)/shard_map/jit(cholesky)/cholesky | solution.py:52
  301.8 2.3 convolution_subtract_fusion.9
  304.1 12.1 %cholesky.524 = f32[128,128]{1,0:T(8,128)S(1)} custom-call(f32[128,128]{1,0:T(8,128)S(1)} %cholesky.601), custom_call_target="Cholesky" | custom-call | tf_op jit(solution)/shard_map/jit(cholesky)/cholesky | solution.py:52
  317.6 9.8 %custom-call.68 = f32[1,128,128]{1,2,0:T(8,128)S(1)} custom-call(f32[1,128,128]{2,1,0:T(8,128)S(1)} %get-tuple-element.55), custom_call_target="InvertDiagBlocksLowerTriangular" | custom-call | tf_op jit(solution)/shard_map/jit(cholesky)/cholesky | solution.py:52
  330.4 11.7 %cholesky.544 = f32[128,128]{1,0:T(8,128)S(1)} custom-call(f32[128,128]{1,0:T(8,128)S(1)} %cholesky.606), custom_call_target="Cholesky" | custom-call | tf_op jit(solution)/shard_map/jit(cholesky)/cholesky | solution.py:52
  343.4 9.8 %custom-call.69 = f32[1,128,128]{1,2,0:T(8,128)S(1)} custom-call(f32[1,128,128]{2,1,0:T(8,128)S(1)} %get-tuple-element.52), custom_call_target="InvertDiagBlocksLowerTriangular" | custom-call | tf_op jit(solution)/shard_map/jit(cholesky)/cholesky | solution.py:52
  355.9 11.9 %cholesky.562 = f32[128,128]{1,0:T(8,128)S(1)} custom-call(f32[128,128]{1,0:T(8,128)S(1)} %convolution_subtract_fusion.11), custom_call_target="Cholesky" | custom-call | tf_op jit(solution)/shard_map/jit(cholesky)/cholesky | solution.py:52
  374.8 4.8 select_select_fusion
  379.7 22.5 %while.1 = (s32[]{:T(128)}, f32[1024,1024]{1,0:T(8,128)}, s32[8,2]{0,1:T(2,128)S(1)}, f32[8,128,128]{2,1,0:T(8,128)S(1)}, s32[]{:T(128)}) while((s32[]{:T(128)}, f32[1024,1024]{1,0:T(8,128)}, s32[8,2]{0,1:T(2,128)S(1)}, f32[8,128,128]{2,1,0:T(8,128)S(1)}, s32[]{:T(128)}) %tuple.62), condition=%wide.while_cond, body=%wide.while_body.sunk | while | flops 2 | bytes 131189 | solution.py:53
  380.3 2.2 bitcast_dynamic-update-slice_fusion.2
  383.1 2.2 bitcast_dynamic-update-slice_fusion.2
  402.1 78.6 %custom-call.70 = f32[8,128,128]{1,2,0:T(8,128)S(1)} custom-call(f32[8,128,128]{2,1,0:T(8,128)S(1)} %get-tuple-element.10), custom_call_target="InvertDiagBlocksLowerTriangular" | custom-call | tf_op jit(solution)/shard_map/jit(_solve_triangular)/triangular_solve | solution.py:53
  491.5 2.2 fusion.39
  495.9 2.6 convolution_subtract_fusion.2
  500.0 2.8 convolution_subtract_fusion.1
  504.3 3.5 convolution_subtract_fusion.3
  509.1 10.6 %multiply_convert_fusion = bf16[1024,1024]{1,0:T(8,128)(2,1)} fusion(bf16[1024,1024]{1,0:T(8,128)(2,1)} %fusion.42, f32[]{:T(128)} %bitcast.7, f32[]{:T(128)} %bitcast.2, bf16[1,2,1024,1024]{3,2,1,0:T(8,128)(2,1)} %param.10), kind=kOutput, calls=%fused_computation.4 | convolution fusion | flops 4304404480 | bytes 10486784 | tf_op jit(solution)/shard_map/dot_general | solution.py:59
  519.7 34.8 %all_to_all.31 = bf16[32,32,1024]{2,1,0:T(8,128)(2,1)S(1)} all-to-all(bf16[32,32,1024]{2,1,0:T(8,128)(2,1)} %bitcast.184), channel_id=1, replica_groups=mesh['sector'=4,'ops_0'=4,'ops_1'=4,'ops_2'=2] {'ops_0','ops_1','ops_2'}, dimensions={0} | all-to-all | bytes 4194304 | tf_op jit(solution)/shard_map/all_to_all | solution.py:67
  555.6 6.5 %all-to-all-start.5 = ((bf16[4,32,1024]{2,1,0:T(8,128)(2,1)}), bf16[4,32,1024]{2,1,0:T(8,128)(2,1)S(1)}, u32[]{:S(2)}, u32[]{:S(2)}) async-start(bf16[4,32,1024]{2,1,0:T(8,128)(2,1)} %broadcast_in_dim.68), calls=%async_computation.5 | async-start | bytes 524288 | tf_op jit(solution)/shard_map/all_to_all | solution.py:12
  564.0 4.8 all-to-all-done.5
  (108 shorter events, 75.7 us)
Async XLA Ops:
  0.6 13.0 %copy-start.6 = (f32[16]{0:T(128)S(1)}, f32[16]{0:T(128)}, u32[]{:S(2)}) copy-start(f32[16]{0:T(128)} %param.13) | copy-start | bytes 196
  0.6 13.0 %copy-start.7 = (s32[1,2]{1,0:T(1,128)S(1)}, s32[1,2]{1,0:T(1,128)}, u32[]{:S(2)}) copy-start(s32[1,2]{1,0:T(1,128)} %param.12) | copy-start | bytes 28
  3.9 37.4 %all-to-all-start = ((bf16[32,32,1024]{2,1,0:T(8,128)(2,1)}), bf16[32,32,1024]{2,1,0:T(8,128)(2,1)S(1)}, u32[]{:S(2)}, u32[]{:S(2)}) async-start(bf16[32,32,1024]{2,1,0:T(8,128)(2,1)} %broadcast_in_dim.62), calls=%async_computation | async-start | bytes 4194304 | tf_op jit(solution)/shard_map/all_to_all | solution.py:12
  76.1 33.1 %copy-start.4 = (bf16[1,32,1024]{2,1,0:T(8,128)(2,1)S(1)}, bf16[1,32,1024]{2,1,0:T(8,128)(2,1)}, u32[]{:S(2)}) copy-start(bf16[1,32,1024]{2,1,0:T(8,128)(2,1)} %param.7) | copy-start | bytes 196612
  76.1 33.1 %copy-start.5 = (f32[1,32,1024]{2,1,0:T(8,128)S(1)}, f32[1,32,1024]{2,1,0:T(8,128)}, u32[]{:S(2)}) copy-start(f32[1,32,1024]{2,1,0:T(8,128)} %param.8) | copy-start | bytes 393220
  76.1 31.1 %all-to-all-start.1 = ((bf16[32,32,1024]{2,1,0:T(8,128)(2,1)}), bf16[32,32,1024]{2,1,0:T(8,128)(2,1)}, u32[]{:S(2)}, u32[]{:S(2)}) async-start(bf16[32,32,1024]{2,1,0:T(8,128)(2,1)} %bitcast.183), calls=%async_computation.1 | async-start | bytes 4194304 | tf_op jit(solution)/shard_map/all_to_all | solution.py:41
  110.9 36.3 %all-to-all-start.3 = ((bf16[32,32,1024]{2,1,0:T(8,128)(2,1)}), bf16[32,32,1024]{2,1,0:T(8,128)(2,1)S(1)}, u32[]{:S(2)}, u32[]{:S(2)}) async-start(bf16[32,32,1024]{2,1,0:T(8,128)(2,1)} %broadcast_in_dim.66), calls=%async_computation.3 | async-start | bytes 4194304 | tf_op jit(solution)/shard_map/all_to_all | solution.py:12
  147.2 2.4 copy-start.3
  149.5 1.9 copy-start
  163.7 2.0 copy-start.2
  480.8 4.4 copy-start.1
  555.6 13.2 %all-to-all-start.5 = ((bf16[4,32,1024]{2,1,0:T(8,128)(2,1)}), bf16[4,32,1024]{2,1,0:T(8,128)(2,1)S(1)}, u32[]{:S(2)}, u32[]{:S(2)}) async-start(bf16[4,32,1024]{2,1,0:T(8,128)(2,1)} %broadcast_in_dim.68), calls=%async_computation.5 | async-start | bytes 524288 | tf_op jit(solution)/shard_map/all_to_all | solution.py:12

commit v2 on v1

--- a/solution.py
+++ b/solution.py
@@ -1,10 +1,147 @@
 import jax
 import jax.numpy as jnp
 from jax import lax
+from jax.experimental import pallas as pl
+from jax.experimental.pallas import tpu as pltpu
 from jax.sharding import Mesh
 from jax.sharding import PartitionSpec as P
 
 OPS = ("ops_0", "ops_1", "ops_2")
+F32, BF16 = jnp.float32, jnp.bfloat16
+NB = 128
+
+
+def two(x):
+    hi = x.astype(BF16)
+    return hi, (x - hi.astype(F32)).astype(BF16)
+
+
+def three(x):
+    hi = x.astype(BF16)
+    rest = x - hi.astype(F32)
+    mid = rest.astype(BF16)
+    return hi, mid, (rest - mid.astype(F32)).astype(BF16)
+
+
+def mm(a, b, dims):
+    return lax.dot_general(a, b, (dims, ((), ())), preferred_element_type=F32)
+
+
+def mm6(a, b, dims):
+    (ah, am, al), (bh, bm, bl) = a, b
+    small = mm(al, bh, dims) + mm(ah, bl, dims) + mm(am, bm, dims)
+    return small + (mm(am, bh, dims) + mm(ah, bm, dims)) + mm(ah, bh, dims)
+
+
+def mm3(a, b, dims):
+    (ah, al), (bh, bl) = a, b
+    return mm(al, bh, dims) + mm(ah, bl, dims) + mm(ah, bh, dims)
+
+
+def wide(x):
+    return jnp.broadcast_to(x, (8, NB))
+
+
+def stacked(rows):
+    at = lax.broadcasted_iota(jnp.int32, (8, NB), 0)
+    out = rows[0]
+    for i in range(1, 8):
+        out = jnp.where(at == i, rows[i], out)
+    return out
+
+
+def inverse_factor(block):
+    panels = NB // 8
+    a = [block[8 * i : 8 * i + 8] for i in range(panels)]
+    row = lax.broadcasted_iota(jnp.int32, (NB, NB), 0)
+    col = lax.broadcasted_iota(jnp.int32, (NB, NB), 1)
+    eye = jnp.where(row == col, F32(1), F32(0))
+    e = [eye[8 * i : 8 * i + 8] for i in range(panels)]
+    done = []
+    for p in range(panels):
+        cols = [wide(a[p][:, 8 * p + j : 8 * p + j + 1]) for j in range(8)]
+        s = {(i, j): wide(cols[j][i : i + 1]) for j in range(8) for i in range(j, 8)}
+        u = [wide(a[p][i : i + 1]) for i in range(8)]
+        w = [wide(e[p][i : i + 1]) for i in range(8)]
+        last = p == panels - 1
+        v = None if last else [wide(a[p + 1][:, 8 * p + j : 8 * p + j + 1]) for j in range(8)]
+        nxt = None if last else a[p + 1]
+        us, ws = [], []
+        for k in range(8):
+            d = s[k, k]
+            r = pl.reciprocal(d, approx=True)
+            r = r * (2.0 - d * r)
+            q = lax.rsqrt(d)
+            q = q * (1.5 - 0.5 * d * (q * q))
+            f = {i: s[i, k] * r for i in range(k + 1, 8)}
+            for i in range(k + 1, 8):
+                for j in range(k + 1, i + 1):
+                    s[i, j] = s[i, j] - f[i] * s[j, k]
+                u[i] = u[i] - f[i] * u[k]
+                w[i] = w[i] - f[i] * w[k]
+                if not last:
+                    v[i] = v[i] - f[i] * v[k]
+            if not last:
+                nxt = nxt - (v[k] * r) * u[k]
+                us.append(u[k] * q)
+            ws.append(w[k] * q)
+        wp = stacked(ws)
+        done.append(wp)
+        if last:
+            break
+        up = stacked(us)
+        a[p + 1] = nxt
+        both = jnp.concatenate([up, wp], axis=1)
+        h = both.astype(BF16).astype(F32)
+        m = (both - h).astype(BF16).astype(F32)
+        t = both - h - m
+        left = jnp.concatenate([x[:, :NB] for x in (h, h, m, m, h, t)], axis=0).astype(BF16)
+        right = jnp.concatenate([h, m, h, m, t, h], axis=0).astype(BF16)
+        out = mm(left, right, ((0,), (0,)))
+        for i in range(p + 1, panels):
+            if i > p + 1:
+                a[i] = a[i] - out[8 * i : 8 * i + 8, :NB]
+            e[i] = e[i] - out[8 * i : 8 * i + 8, NB:]
+    return jnp.concatenate(done, axis=0)
+
+
+def basis_kernel(x_ref, g_ref, b_ref, bl_ref, uh_ref, um_ref, ul_ref, pan_ref):
+    n = x_ref.shape[0]
+    for ref in (b_ref, bl_ref, uh_ref, um_ref, ul_ref):
+        ref[...] = jnp.zeros_like(ref)
+
+    def step(k, carry):
+        at = pl.ds(pl.multiple_of(k * NB, NB), NB)
+        mine = tuple(ref[:, at] for ref in (uh_ref, um_ref, ul_ref))
+        whole = tuple(ref[...] for ref in (uh_ref, um_ref, ul_ref))
+        pan_ref[...] = g_ref[at, :] - mm6(mine, whole, ((0,), (0,)))
+        w = inverse_factor(pan_ref[:, at])
+        u = mm6(three(w), three(pan_ref[...]), ((1,), (0,)))
+        for ref, part in zip((uh_ref, um_ref, ul_ref), three(u)):
+            ref[at, :] = part
+        rest = x_ref[:, at].astype(F32) - mm3(
+            (b_ref[...], bl_ref[...]), (uh_ref[:, at], um_ref[:, at]), ((1,), (0,))
+        )
+        new = mm3(two(rest), two(w), ((1,), (1,)))
+        hi, lo = two(new)
+        b_ref[:, at] = hi
+        bl_ref[:, at] = lo
+        return carry
+
+    lax.fori_loop(0, n // NB, step, 0)
+
+
+def basis_of(x, gram):
+    n = x.shape[0]
+    square = lambda t: pltpu.VMEM((n, n), t)
+    return pl.pallas_call(
+        basis_kernel,
+        out_shape=jax.ShapeDtypeStruct((n, n), BF16),
+        in_specs=[pl.BlockSpec(memory_space=pltpu.VMEM)] * 2,
+        out_specs=pl.BlockSpec(memory_space=pltpu.VMEM),
+        scratch_shapes=[square(BF16)] * 4 + [pltpu.VMEM((NB, n), F32)],
+        compiler_params=pltpu.CompilerParams(vmem_limit_bytes=56 * 2**20),
+    )(x, gram)
 
 
 def from_everyone(x, axis):
@@ -38,20 +175,23 @@
     psi_f = psi.astype(jnp.float32)
     numer_part = jnp.sum(psi_f * total)
     denom = jnp.sum(psi_f * psi_f)
+    high, mid, low = three(numer_part)
+    lane = jnp.arange(NB)
+    tail = jnp.where(lane == 0, high, jnp.where(lane == 1, mid, jnp.where(lane == 2, low, 0)))
+    tail = jnp.broadcast_to(tail.astype(BF16), (order_k, NB))
+    sent = jnp.concatenate([total.astype(BF16), tail], axis=1)
     arrived = lax.all_to_all(
-        total.astype(jnp.bfloat16).reshape(owners, rows_dev, order_k), OPS, 0, 0, tiled=True
-    )
-    numer = jnp.sum(from_everyone(numer_part.reshape(1, 1), OPS))
-    sigma = jnp.sum(arrived.astype(jnp.float32), axis=0)
+        sent.reshape(owners, rows_dev, order_k + NB), OPS, 0, 0, tiled=True
+    ).astype(F32)
+    sigma = jnp.sum(arrived[:, :, :order_k], axis=0)
+    numer = jnp.sum(arrived[:, 0, order_k:])
     energy = numer / denom
     mine = psi_masked.astype(jnp.float32)
     update = mine + (sigma - energy * mine) / diag_scale[0]
     x = from_everyone(update.astype(jnp.bfloat16), OPS).reshape(order_k, order_k)
     gram = lax.dot_general(x, x, (((0,), (0,)), ((), ())), preferred_element_type=jnp.float32)
     gram = gram / order_k + 0.001 * jnp.eye(order_k, dtype=jnp.float32)
-    factor = jnp.linalg.cholesky(gram)
-    basis = jax.scipy.linalg.solve_triangular(factor, x.astype(jnp.float32).T, lower=True).T
-    basis = basis.astype(jnp.bfloat16)
+    basis = basis_of(x, gram)
     mixed = coef[0] * left_ops[0, 0].astype(jnp.float32)
     for p in range(1, left_ops.shape[1]):
         mixed = mixed + coef[p] * left_ops[0, p].astype(jnp.float32)
@@ -66,9 +206,13 @@
     owned = jnp.sum(
         lax.all_to_all(summed, OPS, 0, 0, tiled=True).astype(jnp.float32), axis=0
     )
-    next_rows = jnp.sum(
-        from_everyone(owned.astype(jnp.bfloat16), "sector").astype(jnp.float32), axis=0
-    )
+    owned = owned.astype(BF16)
+    groups = lax.axis_size("sector")
+    near, far, cross = (
+        lax.ppermute(owned, "sector", [(i, i ^ d) for i in range(groups)]).astype(F32)
+        for d in (1, 2, 3)
+    )
+    next_rows = (owned.astype(F32) + near) + (far + cross)
     basis_local = lax.dynamic_slice_in_dim(basis, me * rows_dev, rows_dev, axis=0)
     return (basis_local[None], jnp.reshape(energy, (1,)), next_rows)
 

time: 580 us -> 279 us (0.48); the launches traced: 571 us -> 278 us
  other arithmetic: 272 us -> 10.5 us
  Pallas kernels: 0 us -> 76 us
  matrix products: 83 us -> 35.5 us
  local copies, waits for them, and re-layouts: 45.3 us -> 3.95 us
  blocking collectives: 49.1 us -> 34.6 us
    another operation x33 -> x0, other arithmetic: 256 us -> none  [the longest x30 173 us: shards(): factor = jnp.linalg.cholesky(gram)]
    pallas_call x0 -> x1, Pallas kernels: none -> 76 us  [basis_of(): pl.pallas_call(basis_kernel, out_shape=jax.ShapeDtypeStruct((n, n), BF16)...]
    another operation x29 -> x0, matrix products: 50.3 us -> none  [the longest x15 27.1 us: shards(): jax.scipy.linalg.solve_triangular(factor, x.astype(jnp.float32).T, lower=...]
    all_to_all x1 -> x0, blocking collectives: 34.8 us -> none  [shards(): lax.all_to_all(summed, OPS, 0, 0, tiled=True).astype(jnp.float32)]
    all_to_all x3 -> x1, waiting for transfers between devices: 59.4 us -> 26.9 us  [from_everyone(): lax.all_to_all(jnp.broadcast_to(x[None], (count, *x.shape)), axis, 0, 0,...]
    all_to_all x1 -> x2, waiting for transfers between devices: 22.6 us -> 54.3 us  [the longest x1 27.6 us: shards(): lax.all_to_all(sent.reshape(owners, rows_dev, order_k + NB), OPS, 0, 0, t...]
    another operation x34 -> x0, local copies, waits for them, and re-layouts: 24.9 us -> none
    all_to_all x1, blocking collectives: 14.3 us -> 34.6 us  [from_everyone(): lax.all_to_all(jnp.broadcast_to(x[None], (count, *x.shape)), axis, 0, 0,...]
  transfers between devices with their start and end apart: 4 -> 6, of which waited for: 4 -> 5; matrix products, arithmetic and copies ran while one was open for 1% -> 2% of each run, Pallas kernels for 0% -> 0%
where the time goes in v2:
time: 279 us; the launch traced here: 278 us
  waiting for transfers between devices  83.9 us (30%)
  Pallas kernels  76 us (27%)
  matrix products  35.5 us (13%)
  blocking collectives  34.6 us (12%)
  starting transfers between devices  28.4 us (10%)
  other arithmetic  10.5 us (4%)
  between operations  5.14 us (2%)
  local copies, waits for them, and re-layouts  3.95 us (1%)
    pallas_call x1, Pallas kernels, basis_of(): pl.pallas_call(basis_kernel, out_shape=jax.ShapeDtypeStruct((n, n), BF16)...  76 us
    all_to_all x1, blocking collectives, from_everyone(): lax.all_to_all(jnp.broadcast_to(x[None], (count, *x.shape)), axis, 0, 0,...  34.6 us
    all_to_all x1, waiting for transfers between devices, shards(): lax.all_to_all(sent.reshape(owners, rows_dev, order_k + NB), OPS, 0, 0, t...  27.6 us
    all_to_all x1, waiting for transfers between devices, from_everyone(): lax.all_to_all(jnp.broadcast_to(x[None], (count, *x.shape)), axis, 0, 0,...  26.9 us
    all_to_all x1, waiting for transfers between devices, shards(): lax.all_to_all(summed, OPS, 0, 0, tiled=True).astype(jnp.float32)  26.7 us
    dot_general x2, matrix products, shards(): lax.dot_general(applied.astype(jnp.bfloat16), right_ops[0, p], (((1,), (1...  20.4 us
    dot_general x1, matrix products, shards(): lax.dot_general(basis, moved.astype(jnp.bfloat16), (((0,), (0,)), ((), ()...  10.7 us
    all_to_all x1, starting transfers between devices, from_everyone(): lax.all_to_all(jnp.broadcast_to(x[None], (count, *x.shape)), axis, 0, 0,...  9.73 us
  transfers between devices with their start and end apart: 6, of which 5 were waited for; matrix products, arithmetic and copies ran while one was open for 2% of the time, Pallas kernels for 0%

profile of v2, /device:TPU:1, one launch (start us, length us, event | category | flops | bytes accessed | tf_op | source)
XLA Modules:
  0.0 278.0 jit_solution(12123873240177174957)
XLA Ops:
  0.6 0.0 copy-start.4
  0.6 0.0 copy-start.5
  1.4 0.9 fusion.34
  2.3 1.6 broadcast_in_dim.67
  3.9 9.7 %all-to-all-start = ((bf16[32,32,1024]{2,1,0:T(8,128)(2,1)}), bf16[32,32,1024]{2,1,0:T(8,128)(2,1)S(1)}, u32[]{:S(2)}, u32[]{:S(2)}) async-start(bf16[32,32,1024]{2,1,0:T(8,128)(2,1)} %broadcast_in_dim.67), calls=%async_computation | async-start | bytes 4194304 | tf_op jit(solution)/shard_map/all_to_all | solution.py:149
  13.6 0.0 copy-done.4
  13.6 0.0 copy-done.5
  13.7 0.2 fusion.35
  13.8 0.6 fusion.36
  14.4 26.9 %all-to-all-done = bf16[32,32,1024]{2,1,0:T(8,128)(2,1)S(1)} async-done(((bf16[32,32,1024]{2,1,0:T(8,128)(2,1)}), bf16[32,32,1024]{2,1,0:T(8,128)(2,1)S(1)}, u32[]{:S(2)}, u32[]{:S(2)}) %all-to-all-start) | async-done | bytes 2097184 | tf_op jit(solution)/shard_map/all_to_all | solution.py:149
  41.3 0.0 copy-start
  41.3 9.5 %fusion.6 = f32[1024,1024]{1,0:T(8,128)} fusion(bf16[1,2,1024,1024]{3,2,1,0:T(8,128)(2,1)} %param.11, bf16[1024,1024]{1,0:T(8,128)(2,1)S(1)} %bitcast.75, bf16[1,2,1024,1024]{3,2,1,0:T(8,128)(2,1)} %param.10), kind=kOutput, calls=%fused_computation.15 | convolution fusion | flops 4296015872 | bytes 10485760 | tf_op jit(solution)/shard_map/dot_general | solution.py:167
  50.8 0.0 copy-done
  50.8 11.0 %multiply_reduce_fusion.1 = (f32[]{:T(128)}, bf16[1024,1024]{1,0:T(8,128)(2,1)}) fusion(bf16[32,32,1024]{2,1,0:T(8,128)(2,1)S(1)} %all-to-all-done, bf16[1,2,1024,1024]{3,2,1,0:T(8,128)(2,1)} %param.11, bf16[1024,1024]{1,0:T(8,128)(2,1)S(1)} %bitcast.76, bf16[1,2,1024,1024]{3,2,1,0:T(8,128)(2,1)} %param.10, f32[]{:T(128)} %bitcast.7, ...), kind=kOutput, calls=%fused_computation.7 | convolution fusion | flops 4305453056 | bytes 14683140 | tf_op jit(solution)/shard_map/dot_general | solution.py:167
  63.1 3.5 %pad_maximum_fusion = bf16[1024,1152]{1,0:T(8,128)(2,1)} fusion(bf16[1024,1024]{1,0:T(8,128)(2,1)} %get-tuple-element.4, bf16[1152]{0:T(1024)(128)(2,1)S(1)} %pad.1.clone), kind=kLoop, calls=%fused_computation.9 | loop fusion | flops 4718592 | bytes 4458752 | tf_op jit(solution)/shard_map/concatenate | solution.py:182
  66.6 7.5 %all-to-all-start.1 = ((bf16[32,32,1152]{2,1,0:T(8,128)(2,1)}), bf16[32,32,1152]{2,1,0:T(8,128)(2,1)S(1)}, u32[]{:S(2)}, u32[]{:S(2)}) async-start(bf16[32,32,1152]{2,1,0:T(8,128)(2,1)} %bitcast.74), calls=%async_computation.1 | async-start | bytes 4718592 | tf_op jit(solution)/shard_map/all_to_all | solution.py:183
  74.1 3.3 %multiply_reduce_fusion = f32[]{:T(128)} fusion(bf16[32,32,1024]{2,1,0:T(8,128)(2,1)} %copy-done), kind=kLoop, calls=%fused_computation.6 | loop fusion | flops 3145727 | bytes 2097156 | tf_op jit(solution)/shard_map/reduce_sum | solution.py:177
  77.4 0.0 copy-start.2
  77.4 0.0 copy-start.3
  77.4 27.6 %all-to-all-done.1 = bf16[32,32,1152]{2,1,0:T(8,128)(2,1)S(1)} async-done(((bf16[32,32,1152]{2,1,0:T(8,128)(2,1)}), bf16[32,32,1152]{2,1,0:T(8,128)(2,1)S(1)}, u32[]{:S(2)}, u32[]{:S(2)}) %all-to-all-start.1) | async-done | bytes 2359328 | tf_op jit(solution)/shard_map/all_to_all | solution.py:183
  105.0 0.6 convert_element_type.85
  105.6 0.6 slice_reduce_fusion.1
  106.2 0.2 slice_reduce_fusion
  107.7 0.0 copy-done.2
  107.7 0.0 copy-done.3
  107.7 0.1 fusion.33
  107.8 0.2 broadcast_in_dim.75
  108.1 34.6 %all_to_all.20 = bf16[32,32,1024]{2,1,0:T(8,128)(2,1)S(1)} all-to-all(bf16[32,32,1024]{2,1,0:T(8,128)(2,1)S(1)} %broadcast_in_dim.75), channel_id=1, replica_groups=mesh['sector'=4,'ops_0'=4,'ops_1'=4,'ops_2'=2] {'ops_0','ops_1','ops_2'}, dimensions={0} | all-to-all | bytes 4194304 | tf_op jit(solution)/shard_map/all_to_all | solution.py:149
  142.7 0.0 copy-start.1
  142.7 4.4 %fusion.g_ref = f32[1024,1024]{1,0:T(8,128)} fusion(bf16[32,32,1024]{2,1,0:T(8,128)(2,1)S(1)} %all_to_all.20), kind=kOutput, calls=%fused_computation.2 | convolution fusion | flops 2151677952 | bytes 6291456 | tf_op jit(solution)/shard_map/dot_general | solution.py:192
  147.0 0.0 copy-done.1
  147.0 76.0 %shard_map.94 = bf16[1024,1024]{1,0:T(8,128)(2,1)} custom-call(bf16[1024,1024]{1,0:T(8,128)(2,1)} %bitcast.77, f32[1024,1024]{1,0:T(8,128)} %fusion.g_ref), custom_call_target="tpu_custom_call" | custom-call | tf_op jit(solution)/shard_map/pallas_call | solution.py:137
  223.1 10.7 %multiply_convert_fusion = bf16[1024,1024]{1,0:T(8,128)(2,1)} fusion(bf16[1024,1024]{1,0:T(8,128)(2,1)} %shard_map.94, f32[]{:T(128)} %bitcast.7, f32[]{:T(128)} %bitcast.2, bf16[1,2,1024,1024]{3,2,1,0:T(8,128)(2,1)} %param.10), kind=kOutput, calls=%fused_computation.3 | convolution fusion | flops 4304404480 | bytes 10486784 | tf_op jit(solution)/shard_map/dot_general | solution.py:199
  233.7 5.4 %all-to-all-start.3 = ((bf16[32,32,1024]{2,1,0:T(8,128)(2,1)}), bf16[32,32,1024]{2,1,0:T(8,128)(2,1)S(1)}, u32[]{:S(2)}, u32[]{:S(2)}) async-start(bf16[32,32,1024]{2,1,0:T(8,128)(2,1)} %bitcast.78), calls=%async_computation.3 | async-start | bytes 4194304 | tf_op jit(solution)/shard_map/all_to_all | solution.py:207
  239.2 26.7 %all-to-all-done.3 = bf16[32,32,1024]{2,1,0:T(8,128)(2,1)S(1)} async-done(((bf16[32,32,1024]{2,1,0:T(8,128)(2,1)}), bf16[32,32,1024]{2,1,0:T(8,128)(2,1)S(1)}, u32[]{:S(2)}, u32[]{:S(2)}) %all-to-all-start.3) | async-done | bytes 2097184 | tf_op jit(solution)/shard_map/all_to_all | solution.py:207
  265.9 0.4 reduce_sum.65
  266.3 5.3 %collective-permute-start.2 = (bf16[32,1024]{1,0:T(8,128)(2,1)S(1)}, bf16[32,1024]{1,0:T(8,128)(2,1)S(1)}, u32[]{:S(2)}, u32[]{:S(2)}) collective-permute-start(bf16[32,1024]{1,0:T(8,128)(2,1)S(1)} %reduce_sum.65), channel_id=1, source_target_pairs={{0,96},{32,64},{64,32},{96,0},{1,97},{33,65},{65,33},{97,1},{2,98}... | collective-permute-start | bytes 196616 | tf_op jit(solution)/shard_map/ppermute | solution.py:212
  271.5 0.4 collective-permute-start.1
  271.9 0.1 collective-permute-start
  272.0 1.5 dynamic-slice_bitcast_fusion
  273.5 0.9 collective-permute-done.2
  274.4 1.7 collective-permute-done.1
  276.2 0.0 collective-permute-done
  276.2 0.7 add_add_fusion
  (4 shorter events, 0.0 us)
Async XLA Ops:
  0.6 13.0 %copy-start.4 = (f32[16]{0:T(128)S(1)}, f32[16]{0:T(128)}, u32[]{:S(2)}) copy-start(f32[16]{0:T(128)} %param.13) | copy-start | bytes 196
  0.6 13.0 %copy-start.5 = (s32[1,2]{1,0:T(1,128)S(1)}, s32[1,2]{1,0:T(1,128)}, u32[]{:S(2)}) copy-start(s32[1,2]{1,0:T(1,128)} %param.12) | copy-start | bytes 28
  3.9 37.4 %all-to-all-start = ((bf16[32,32,1024]{2,1,0:T(8,128)(2,1)}), bf16[32,32,1024]{2,1,0:T(8,128)(2,1)S(1)}, u32[]{:S(2)}, u32[]{:S(2)}) async-start(bf16[32,32,1024]{2,1,0:T(8,128)(2,1)} %broadcast_in_dim.67), calls=%async_computation | async-start | bytes 4194304 | tf_op jit(solution)/shard_map/all_to_all | solution.py:149
  41.3 9.5 %copy-start = (bf16[32,32,1024]{2,1,0:T(8,128)(2,1)}, bf16[32,32,1024]{2,1,0:T(8,128)(2,1)S(1)}, u32[]{:S(2)}) copy-start(bf16[32,32,1024]{2,1,0:T(8,128)(2,1)S(1)} %all-to-all-done) | copy-start | bytes 6291460
  66.6 38.4 %all-to-all-start.1 = ((bf16[32,32,1152]{2,1,0:T(8,128)(2,1)}), bf16[32,32,1152]{2,1,0:T(8,128)(2,1)S(1)}, u32[]{:S(2)}, u32[]{:S(2)}) async-start(bf16[32,32,1152]{2,1,0:T(8,128)(2,1)} %bitcast.74), calls=%async_computation.1 | async-start | bytes 4718592 | tf_op jit(solution)/shard_map/all_to_all | solution.py:183
  77.4 30.3 %copy-start.2 = (bf16[1,32,1024]{2,1,0:T(8,128)(2,1)S(1)}, bf16[1,32,1024]{2,1,0:T(8,128)(2,1)}, u32[]{:S(2)}) copy-start(bf16[1,32,1024]{2,1,0:T(8,128)(2,1)} %param.7) | copy-start | bytes 196612
  77.4 30.3 %copy-start.3 = (f32[1,32,1024]{2,1,0:T(8,128)S(1)}, f32[1,32,1024]{2,1,0:T(8,128)}, u32[]{:S(2)}) copy-start(f32[1,32,1024]{2,1,0:T(8,128)} %param.8) | copy-start | bytes 393220
  142.7 4.4 %copy-start.1 = (bf16[32,32,1024]{2,1,0:T(8,128)(2,1)}, bf16[32,32,1024]{2,1,0:T(8,128)(2,1)S(1)}, u32[]{:S(2)}) copy-start(bf16[32,32,1024]{2,1,0:T(8,128)(2,1)S(1)} %all_to_all.20) | copy-start | bytes 6291460
  233.7 32.1 %all-to-all-start.3 = ((bf16[32,32,1024]{2,1,0:T(8,128)(2,1)}), bf16[32,32,1024]{2,1,0:T(8,128)(2,1)S(1)}, u32[]{:S(2)}, u32[]{:S(2)}) async-start(bf16[32,32,1024]{2,1,0:T(8,128)(2,1)} %bitcast.78), calls=%async_computation.3 | async-start | bytes 4194304 | tf_op jit(solution)/shard_map/all_to_all | solution.py:207
  266.3 8.2 %collective-permute-start.2 = (bf16[32,1024]{1,0:T(8,128)(2,1)S(1)}, bf16[32,1024]{1,0:T(8,128)(2,1)S(1)}, u32[]{:S(2)}, u32[]{:S(2)}) collective-permute-start(bf16[32,1024]{1,0:T(8,128)(2,1)S(1)} %reduce_sum.65), channel_id=1, source_target_pairs={{0,96},{32,64},{64,32},{96,0},{1,97},{33,65},{65,33},{97,1},{2,98}... | collective-permute-start | bytes 196616 | tf_op jit(solution)/shard_map/ppermute | solution.py:212
  271.5 4.6 %collective-permute-start.1 = (bf16[32,1024]{1,0:T(8,128)(2,1)S(1)}, bf16[32,1024]{1,0:T(8,128)(2,1)S(1)}, u32[]{:S(2)}, u32[]{:S(2)}) collective-permute-start(bf16[32,1024]{1,0:T(8,128)(2,1)S(1)} %reduce_sum.65), channel_id=1, source_target_pairs={{0,64},{32,96},{64,0},{96,32},{1,65},{33,97},{65,1},{97,33},{2,66}... | collective-permute-start | bytes 196616 | tf_op jit(solution)/shard_map/ppermute | solution.py:212
  271.9 4.3 %collective-permute-start = (bf16[32,1024]{1,0:T(8,128)(2,1)S(1)}, bf16[32,1024]{1,0:T(8,128)(2,1)S(1)}, u32[]{:S(2)}, u32[]{:S(2)}) collective-permute-start(bf16[32,1024]{1,0:T(8,128)(2,1)S(1)} %reduce_sum.65), channel_id=1, source_target_pairs={{0,32},{32,0},{64,96},{96,64},{1,33},{33,1},{65,97},{97,65},{2,34}... | collective-permute-start | bytes 196616 | tf_op jit(solution)/shard_map/ppermute | solution.py:212

commit v3 on v2

v3 whole, which is shorter than its diff:
```python
import jax
import jax.numpy as jnp
from jax import lax
from jax.experimental import pallas as pl
from jax.experimental.pallas import tpu as pltpu
from jax.sharding import Mesh
from jax.sharding import PartitionSpec as P

OPS = ("ops_0", "ops_1", "ops_2")
F32, BF16 = jnp.float32, jnp.bfloat16
NB = 128


def two(x):
    hi = x.astype(BF16)
    return hi, (x - hi.astype(F32)).astype(BF16)


def three(x):
    hi = x.astype(BF16)
    rest = x - hi.astype(F32)
    mid = rest.astype(BF16)
    return hi, mid, (rest - mid.astype(F32)).astype(BF16)


def mm(a, b, dims):
    return lax.dot_general(a, b, (dims, ((), ())), preferred_element_type=F32)


def mm6(a, b, dims):
    (ah, am, al), (bh, bm, bl) = a, b
    small = mm(al, bh, dims) + mm(ah, bl, dims) + mm(am, bm, dims)
    return small + (mm(am, bh, dims) + mm(ah, bm, dims)) + mm(ah, bh, dims)


def mm3(a, b, dims):
    (ah, al), (bh, bl) = a, b
    return mm(al, bh, dims) + mm(ah, bl, dims) + mm(ah, bh, dims)


def wide(x):
    return jnp.broadcast_to(x, (8, NB))


def stacked(rows):
    at = lax.broadcasted_iota(jnp.int32, (8, NB), 0)
    out = rows[0]
    for i in range(1, 8):
        out = jnp.where(at == i, rows[i], out)
    return out


def inv_sqrt(d):
    q = lax.rsqrt(d)
    return q * (1.5 - 0.5 * d * (q * q))


def inverse_factor(block):
    panels = NB // 8
    a = [block[8 * i : 8 * i + 8] for i in range(panels)]
    row = lax.broadcasted_iota(jnp.int32, (NB, NB), 0)
    col = lax.broadcasted_iota(jnp.int32, (NB, NB), 1)
    eye = jnp.where(row == col, F32(1), F32(0))
    e = [eye[8 * i : 8 * i + 8] for i in range(panels)]
    done = []
    for p in range(panels):
        cols = [wide(a[p][:, 8 * p + j : 8 * p + j + 1]) for j in range(8)]
        s = {(i, j): wide(cols[j][i : i + 1]) for j in range(8) for i in range(j, 8)}
        u = [wide(a[p][i : i + 1]) for i in range(8)]
        w = [wide(e[p][i : i + 1]) for i in range(8)]
        last = p == panels - 1
        v = None if last else [wide(a[p + 1][:, 8 * p + j : 8 * p + j + 1]) for j in range(8)]
        nxt = None if last else a[p + 1]
        us, ws = [], []
        for k in range(0, 8, 2):
            d0, c, d1 = s[k, k], s[k + 1, k], s[k + 1, k + 1]
            det = d0 * d1 - c * c
            rd = pl.reciprocal(det, approx=True)
            rd = rd * (2.0 - det * rd)
            r0 = pl.reciprocal(d0, approx=True)
            r0 = r0 * (2.0 - d0 * r0)
            q0, q1 = inv_sqrt(d0), inv_sqrt(det * r0)
            f0, f1 = {}, {}
            for i in range(k + 2, 8):
                f0[i] = (s[i, k] * d1 - s[i, k + 1] * c) * rd
                f1[i] = (s[i, k + 1] * d0 - s[i, k] * c) * rd
            for i in range(k + 2, 8):
                for j in range(k + 2, i + 1):
                    s[i, j] = s[i, j] - (f0[i] * s[j, k] + f1[i] * s[j, k + 1])
            g = c * r0

            def swept(rows):
                for i in range(k + 2, 8):
                    rows[i] = rows[i] - (f0[i] * rows[k] + f1[i] * rows[k + 1])
                return rows[k] * q0, (rows[k + 1] - g * rows[k]) * q1

            ws.extend(swept(w))
            if not last:
                u0, u1 = swept(u)
                v0, v1 = swept(v)
                nxt = nxt - (v0 * u0 + v1 * u1)
                us.extend((u0, u1))
        wp = stacked(ws)
        done.append(wp)
        if last:
            break
        up = stacked(us)
        a[p + 1] = nxt
        both = jnp.concatenate([up, wp], axis=1)
        h = both.astype(BF16).astype(F32)
        m = (both - h).astype(BF16).astype(F32)
        t = both - h - m
        left = jnp.concatenate([x[:, :NB] for x in (h, h, m, m, h, t)], axis=0).astype(BF16)
        right = jnp.concatenate([h, m, h, m, t, h], axis=0).astype(BF16)
        out = mm(left, right, ((0,), (0,)))
        for i in range(p + 1, panels):
            if i > p + 1:
                a[i] = a[i] - out[8 * i : 8 * i + 8, :NB]
            e[i] = e[i] - out[8 * i : 8 * i + 8, NB:]
    return jnp.concatenate(done, axis=0)


def factor_half(g_ref, x_ref, bh_ref, bm_ref, u_refs, w_ref, pan_ref, ready=None):
    half = g_ref.shape[0]

    def parts(rows, cols):
        return tuple(ref[rows, cols] for ref in u_refs)

    def step(k, carry):
        for j in range(half // NB):
            lo = NB * j

            @pl.when(k == j)
            def _():
                acc = g_ref[lo : lo + NB, lo:]
                if j:
                    above = slice(0, lo)
                    acc = acc - mm6(
                        parts(above, slice(lo, lo + NB)), parts(above, slice(lo, half)), ((0,), (0,))
                    )
                pan_ref[:, : half - lo] = acc

        w_ref[pl.ds(pl.multiple_of(k * NB, NB), NB), :] = inverse_factor(pan_ref[:, :NB])
        for j in range(half // NB):
            lo = NB * j

            @pl.when(k == j)
            def _():
                w = w_ref[lo : lo + NB, :]
                u = mm6(three(w), three(pan_ref[:, : half - lo]), ((1,), (0,)))
                for ref, part in zip(u_refs, three(u)):
                    ref[lo : lo + NB, lo:] = part
                if ready is not None:
                    ready(j, False)
                if j % 2:
                    c, hi = lo - NB, lo + NB
                    above, pair = slice(0, c), slice(c, hi)
                    rest = x_ref[:, pair].astype(F32)
                    if c:
                        rest = rest - mm3(
                            (bh_ref[:, above], bm_ref[:, above]), parts(above, pair)[:2], ((1,), (0,))
                        )
                    first = w_ref[c:lo, :]
                    cross = mm6(parts(slice(c, lo), slice(lo, hi)), three(first), ((0,), (0,)))
                    cross = mm6(three(w), three(cross), ((1,), (0,)))
                    both = jnp.concatenate(
                        [
                            jnp.concatenate([first, jnp.zeros_like(first)], axis=1),
                            jnp.concatenate([-cross, w], axis=1),
                        ],
                        axis=0,
                    )
                    new = mm3(two(rest), two(both), ((1,), (1,)))
                    bh_ref[:, pair], bm_ref[:, pair] = two(new)
                    if ready is not None:
                        ready(j, True)

        return carry

    lax.fori_loop(0, half // NB, step, 0)


def gram_of(x, n):
    half = x.shape[1]
    row = lax.broadcasted_iota(jnp.int32, (half, half), 0)
    col = lax.broadcasted_iota(jnp.int32, (half, half), 1)
    return mm(x, x, ((0,), (0,))) * (1.0 / n) + jnp.where(row == col, F32(0.001), F32(0))


def first_kernel(x_ref, *refs):
    out, held, (g_ref, pan_ref, sems) = refs[:6], refs[6:12], refs[12:]
    bh_ref, bm_ref, uh_ref, um_ref, ul_ref, w_ref = held
    half = x_ref.shape[1]

    def pieces(j, basis):
        rows = slice(NB * j, NB * (j + 1))
        pair = slice(NB * (j - 1), NB * (j + 1))
        if basis:
            which = [(i, (slice(None), pair)) for i in (0, 1)]
        else:
            which = [(i, (rows, slice(NB * j, half))) for i in (2, 3, 4)] + [(5, (rows, slice(None)))]
        return [pltpu.make_async_copy(held[i].at[at], out[i].at[at], sems.at[i, j]) for i, at in which]

    def send(j, basis):
        for copy in pieces(j, basis):
            copy.start()

    g_ref[...] = gram_of(x_ref[...], x_ref.shape[0])
    factor_half(g_ref, x_ref, bh_ref, bm_ref, (uh_ref, um_ref, ul_ref), w_ref, pan_ref, send)
    for j in range(half // NB):
        for copy in pieces(j, False) + (pieces(j, True) if j % 2 else []):
            copy.wait()


def second_kernel(place_ref, *refs):
    given, (rows_ref, give_ref, keep_ref), held, rest = refs[:9], refs[9:12], refs[12:20], refs[20:]
    basis_ref, bm_ref, uh_ref, um_ref, ul_ref, vh_ref, vm_ref, vl_ref = rest[:8]
    w_ref, g_ref, x_ref, pan_ref, moved_ref, sems = rest[8:]
    x2_ref, x1_ref, w1_ref, u1h_ref, u1m_ref, u1l_ref, b1m_ref, mixed_ref = held
    n, half = x2_ref.shape
    left, right = (basis_ref.at[:, slice(c, c + half)] for c in (0, half))
    copies = [
        pltpu.make_async_copy(a, b, sems.at[i]) for i, (a, b) in enumerate(zip(given, (*held[:7], left, held[7])))
    ]
    for copy in copies:
        copy.start()
    u1 = (u1h_ref, u1m_ref, u1l_ref)
    cross = (vh_ref, vm_ref, vl_ref)
    copies[0].wait()
    x2 = x2_ref[...]
    g_ref[...] = gram_of(x2, n)
    for copy in copies[1:6]:
        copy.wait()
    for j in range(half // NB):
        lo = NB * j
        mine = slice(lo, lo + NB)
        acc = mm(x1_ref[:, mine], x2, ((0,), (0,))) * (1.0 / n)
        if j:
            acc = acc - mm6(
                tuple(ref[:lo, mine] for ref in u1), tuple(ref[:lo, :] for ref in cross), ((0,), (0,))
            )
        for ref, part in zip(cross, three(mm6(three(w1_ref[mine, :]), three(acc), ((1,), (0,))))):
            ref[mine, :] = part
    whole = tuple(ref[...] for ref in cross)
    g_ref[...] = g_ref[...] - mm6(whole, whole, ((0,), (0,)))
    for copy in copies[6:8]:
        copy.wait()
    x_ref[...] = x2.astype(F32) - mm3((basis_ref[:, :half], b1m_ref[...]), whole[:2], ((1,), (0,)))
    factor_half(g_ref, x_ref, right, bm_ref, (uh_ref, um_ref, ul_ref), w_ref, pan_ref)
    me, core = place_ref[0], place_ref[1]
    own = rows_ref.shape[0]
    rows_ref[...] = basis_ref[pl.ds(pl.multiple_of(me * own, own), own), :]
    copies[8].wait()
    moved_ref[...] = mm(mixed_ref[...], basis_ref[...], ((1,), (0,))).astype(BF16)
    for ref, side in ((give_ref, 1 - core), (keep_ref, core)):
        cols = moved_ref[:, pl.ds(pl.multiple_of(side * half, half), half)]
        ref[...] = (mm(basis_ref[...], cols, ((0,), (0,))) * (1.0 / n)).astype(BF16)


VMEM = pl.BlockSpec(memory_space=pltpu.VMEM)
SMEM = pl.BlockSpec(memory_space=pltpu.SMEM)
HBM = pl.BlockSpec(memory_space=pltpu.HBM)


def basis_and_rotation(x1, x2, mixed, place, own):
    n, half = x1.shape
    sds = jax.ShapeDtypeStruct
    tall, square = sds((n, half), BF16), sds((half, half), BF16)
    strip = sds((half, NB), F32)
    params = pltpu.CompilerParams(vmem_limit_bytes=60 * 2**20)
    g, pan = pltpu.VMEM((half, half), F32), pltpu.VMEM((NB, half), F32)
    out = [tall, tall, square, square, square, strip]
    bh, bm, uh, um, ul, w = pl.pallas_call(
        first_kernel,
        out_shape=out,
        in_specs=[VMEM],
        out_specs=[HBM] * len(out),
        scratch_shapes=[pltpu.VMEM(a.shape, a.dtype) for a in out]
        + [g, pan, pltpu.SemaphoreType.DMA((len(out), half // NB))],
        compiler_params=params,
    )(x1)
    operands = (x2, x1, w, uh, um, ul, bm, bh, mixed)
    waiting = operands[:7] + operands[8:]
    quarter = sds((n, half), BF16)
    return pl.pallas_call(
        second_kernel,
        out_shape=[sds((own, n), BF16), quarter, quarter],
        in_specs=[SMEM] + [HBM] * len(operands),
        out_specs=[VMEM] * 3,
        scratch_shapes=[pltpu.VMEM(a.shape, a.dtype) for a in waiting]
        + [pltpu.VMEM((n, n), BF16), pltpu.VMEM((n, half), BF16)]
        + [pltpu.VMEM((half, half), BF16)] * 6
        + [pltpu.VMEM((half, NB), F32), g, pltpu.VMEM((n, half), F32), pan]
        + [pltpu.VMEM((n, n), BF16), pltpu.SemaphoreType.DMA((len(operands),))],
        compiler_params=params,
    )(place, *operands)


def sigma_kernel(
    coef_ref, dim_ref, psi_ref, left_hbm, right_hbm, sent_ref, denom_ref, mixed_hbm,
    app_ref, left_ref, right_ref, mixed_ref, sems,
):
    n = psi_ref.shape[0]
    step = 256
    count = left_ref.shape[0]
    pairs = range(count)
    dim = dim_ref[0]
    blocks = [(p, slice(r, r + n // 2)) for p in pairs for r in (0, n // 2)]

    def fetch(source, held, at):
        return [
            pltpu.make_async_copy(source.at[0, p, rows, :], held.at[p, rows, :], sems.at[at, i])
            for i, (p, rows) in enumerate(blocks)
        ]

    lefts, rights = fetch(left_hbm, left_ref, 0), fetch(right_hbm, right_ref, 1)
    for copy in lefts + rights:
        copy.start()
    for copy, (p, rows) in zip(lefts, blocks):
        copy.wait()
        app_ref[p, rows, :] = mm(left_ref[p, rows, :], psi_ref[...], ((1,), (0,))).astype(BF16)
    for copy in rights:
        copy.wait()
    mixed = coef_ref[0] * left_ref[0].astype(F32)
    for p in pairs[1:]:
        mixed = mixed + coef_ref[p] * left_ref[p].astype(F32)
    mixed_ref[...] = mixed.astype(BF16)
    put = pltpu.make_async_copy(mixed_ref, mixed_hbm, sems.at[2, 0])
    put.start()
    row = lax.broadcasted_iota(jnp.int32, (n, step), 0)
    numer, denom = F32(0), F32(0)
    for c in range(0, n, step):
        cols = slice(c, c + step)
        total = jnp.zeros((n, step), F32)
        for p in pairs:
            total = total + coef_ref[p] * mm(app_ref[p], right_ref[p, cols, :], ((1,), (1,)))
        col = lax.broadcasted_iota(jnp.int32, (n, step), 1) + c
        total = jnp.where((row < dim) & (col < dim), total, F32(0))
        psi = psi_ref[:, cols].astype(F32)
        numer = numer + jnp.sum(psi * total)
        denom = denom + jnp.sum(psi * psi)
        sent_ref[:, cols] = total.astype(BF16)
    lane = lax.broadcasted_iota(jnp.int32, (n, NB), 1)
    numer = jnp.full((n, NB), numer, F32)
    high, mid, low = (part.astype(F32) for part in three(numer))
    tail = jnp.where(lane == 0, high, jnp.where(lane == 1, mid, jnp.where(lane == 2, low, F32(0))))
    sent_ref[:, n:] = tail.astype(BF16)
    denom_ref[0] = denom
    put.wait()


def sigma_part(coef, dim, psi, left_ops, right_ops):
    n = psi.shape[0]
    sds = jax.ShapeDtypeStruct
    return pl.pallas_call(
        sigma_kernel,
        out_shape=[sds((n, n + NB), BF16), sds((1,), F32), sds((n, n), BF16)],
        in_specs=[SMEM, SMEM, VMEM, HBM, HBM],
        out_specs=[VMEM, SMEM, HBM],
        scratch_shapes=[pltpu.VMEM(left_ops.shape[1:], BF16)] * 3
        + [pltpu.VMEM((n, n), BF16), pltpu.SemaphoreType.DMA((3, 2 * left_ops.shape[1]))],
        compiler_params=pltpu.CompilerParams(vmem_limit_bytes=58 * 2**20),
    )(coef, dim, psi, left_ops, right_ops)


def from_everyone(x, axis):
    count = lax.axis_size(axis)
    return lax.all_to_all(jnp.broadcast_to(x[None], (count, *x.shape)), axis, 0, 0, tiled=True)


def rows_of_all(x):
    got = from_everyone(x, OPS)
    return got.reshape(-1, got.shape[-1])


def to_owners(x):
    tiles = x.reshape(lax.axis_size(OPS), -1, x.shape[-1])
    return lax.all_to_all(tiles, OPS, 0, 0, tiled=True).astype(F32)


def shards(wavefunction, diag_scale, sector_dims, left_ops, right_ops, weight_index, weight_table):
    psi_local = wavefunction[0]
    rows_dev, order_k = psi_local.shape
    half = order_k // 2
    me = lax.axis_index(OPS)
    dim = sector_dims[0]
    live = jnp.arange(order_k) < dim
    row_live = me * rows_dev + jnp.arange(rows_dev) < dim
    mine = jnp.where(row_live[:, None] & live[None, :], psi_local, BF16(0))
    psi = rows_of_all(mine)
    onehot = weight_index[0][:, None] == jnp.arange(weight_table.shape[0])[None, :]
    coef = jnp.sum(jnp.where(onehot, weight_table[None, :], F32(0)), axis=1)
    sent, denom, mixed = sigma_part(coef, sector_dims, psi, left_ops, right_ops)
    arrived = to_owners(sent)
    sigma = jnp.sum(arrived[:, :, :order_k], axis=0)
    energy = jnp.sum(arrived[:, 0, order_k:]) / denom[0]
    old = mine.astype(F32)
    update = (old + (sigma - energy * old) / diag_scale[0]).astype(BF16)
    x = [rows_of_all(update[:, h]) for h in (slice(0, half), slice(half, order_k))]
    core = lax.axis_index("sector") % 2
    place = jnp.stack([me, core]).astype(jnp.int32)
    basis_local, give, keep = basis_and_rotation(*x, mixed, place, rows_dev)

    def swapped(values, bits):
        count = lax.axis_size("sector")
        return lax.ppermute(values, "sector", [(i, i ^ bits) for i in range(count)])

    kept = (keep.astype(F32) + swapped(give, 1).astype(F32)).astype(BF16)
    owned = jnp.sum(to_owners(kept), axis=0).astype(BF16)
    near, far, cross = (swapped(owned, bits).astype(F32) for bits in (1, 2, 3))
    own, other = owned.astype(F32) + far, near + cross
    next_rows = jnp.concatenate(
        [jnp.where(core == 0, own, other), jnp.where(core == 0, other, own)], axis=1
    )
    return (basis_local[None], jnp.reshape(energy, (1,)), next_rows)


def solution(mesh):
    split = Mesh(
        mesh.devices.reshape(mesh.shape["sector"], 4, 4, 2), ("sector", "ops_0", "ops_1", "ops_2")
    )
    in_specs = (
        P("sector", OPS, None),
        P("sector", OPS, None),
        P("sector"),
        P("sector", OPS, None, None),
        P("sector", OPS, None, None),
        P("sector", OPS),
        P(),
    )
    out_specs = (P("sector", OPS, None), P("sector"), P(OPS, None))
    return jax.shard_map(
        shards, mesh=split, in_specs=in_specs, out_specs=out_specs, check_vma=False
    )
```

time: 279 us -> 231 us (0.83)
  waiting for transfers between devices: 83.9 us -> 33.4 us
  blocking collectives: 34.6 us -> 82.5 us
  matrix products: 35.5 us -> 0 us
  starting transfers between devices: 28.4 us -> 21.8 us
  other arithmetic: 10.5 us -> 6.18 us
    all_to_all x0 -> x2, blocking collectives: none -> 61.7 us  [to_owners(): return lax.all_to_all(tiles, OPS, 0, 0, tiled=True).astype(F32)]
    all_to_all x2 -> x0, waiting for transfers between devices: 54.3 us -> none  [the longest x1 27.6 us: shards(): lax.all_to_all(sent.reshape(owners, rows_dev, order_k + NB), OPS, 0, 0, t...]
    dot_general x4 -> x0, matrix products: 35.5 us -> none  [the longest x2 20.4 us: shards(): lax.dot_general(applied.astype(jnp.bfloat16), right_ops[0, p], (((1,), (1...]
    all_to_all x1, blocking collectives: 34.6 us -> 20.8 us  [from_everyone(): lax.all_to_all(jnp.broadcast_to(x[None], (count, *x.shape)), axis, 0, 0,...]
    all_to_all x2 -> x0, starting transfers between devices: 12.9 us -> none  [the longest x1 7.45 us: shards(): lax.all_to_all(sent.reshape(owners, rows_dev, order_k + NB), OPS, 0, 0, t...]
    all_to_all x1 -> x2, starting transfers between devices: 9.73 us -> 14.6 us  [from_everyone(): lax.all_to_all(jnp.broadcast_to(x[None], (count, *x.shape)), axis, 0, 0,...]
    ppermute x3 -> x4, waiting for transfers between devices: 2.66 us -> 6.42 us  [swapped(): return lax.ppermute(values, 'sector', [(i, i ^ bits) for i in range(count)])]
    reduce_sum x4 -> x3, other arithmetic: 4.46 us -> 1.48 us  [the longest x1 0.69 us: shards(): coef = jnp.sum(jnp.where(onehot, weight_table[None, :], F32(0)), axis=1)]
  transfers between devices with their start and end apart: 6 -> 6, of which waited for: 5 -> 4; matrix products, arithmetic and copies ran while one was open for 2% -> 1% of each run, Pallas kernels for 0% -> 10%
where the time goes in v3:
time: 231 us; the launch traced here: 230 us
  blocking collectives  82.5 us (36%)
  Pallas kernels  76.9 us (33%)
  waiting for transfers between devices  33.4 us (14%)
  starting transfers between devices  21.8 us (9%)
  other arithmetic  6.18 us (3%)
  local copies, waits for them, and re-layouts  5.17 us (2%)
  between operations  3.98 us (2%)
    all_to_all x2, blocking collectives, to_owners(): return lax.all_to_all(tiles, OPS, 0, 0, tiled=True).astype(F32)  61.7 us
    pallas_call x1, Pallas kernels, basis_and_rotation(): pl.pallas_call(second_kernel, out_shape=[sds((own, n), BF16), quarter, qu...  35.8 us
    all_to_all x2, waiting for transfers between devices, from_everyone(): lax.all_to_all(jnp.broadcast_to(x[None], (count, *x.shape)), axis, 0, 0,...  27 us
    pallas_call x1, Pallas kernels, basis_and_rotation(): pl.pallas_call(first_kernel, out_shape=out, in_specs=[VMEM], out_specs=[H...  23.6 us
    all_to_all x1, blocking collectives, from_everyone(): lax.all_to_all(jnp.broadcast_to(x[None], (count, *x.shape)), axis, 0, 0,...  20.8 us
    pallas_call x1, Pallas kernels, sigma_part(): pl.pallas_call(sigma_kernel, out_shape=[sds((n, n + NB), BF16), sds((1,),...  17.5 us
    all_to_all x2, starting transfers between devices, from_everyone(): lax.all_to_all(jnp.broadcast_to(x[None], (count, *x.shape)), axis, 0, 0,...  14.6 us
    ppermute x4, starting transfers between devices, swapped(): return lax.ppermute(values, 'sector', [(i, i ^ bits) for i in range(count)])  7.22 us
  transfers between devices with their start and end apart: 6, of which 4 were waited for; matrix products, arithmetic and copies ran while one was open for 1% of the time, Pallas kernels for 10%

profile of v3, /device:TPU:1, one launch (start us, length us, event | category | flops | bytes accessed | tf_op | source)
XLA Modules:
  0.0 229.9 jit_solution(2916371526324394505)
XLA Ops:
  1.3 0.9 fusion.3
  2.3 1.6 broadcast_in_dim.50
  3.9 0.0 copy-start.4
  3.9 0.0 copy-start.5
  3.9 9.9 %all-to-all-start = ((bf16[32,32,1024]{2,1,0:T(8,128)(2,1)}), bf16[32,32,1024]{2,1,0:T(8,128)(2,1)S(1)}, u32[]{:S(2)}, u32[]{:S(2)}) async-start(bf16[32,32,1024]{2,1,0:T(8,128)(2,1)} %broadcast_in_dim.50), calls=%async_computation | async-start | bytes 4194304 | tf_op jit(solution)/shard_map/all_to_all | solution.py:368
  13.7 0.0 copy-done.4
  13.7 0.0 copy-done.5
  13.8 0.7 fusion.6.coef_ref
  14.4 27.0 %all-to-all-done = bf16[32,32,1024]{2,1,0:T(8,128)(2,1)S(1)} async-done(((bf16[32,32,1024]{2,1,0:T(8,128)(2,1)}), bf16[32,32,1024]{2,1,0:T(8,128)(2,1)S(1)}, u32[]{:S(2)}, u32[]{:S(2)}) %all-to-all-start) | async-done | bytes 2097184 | tf_op jit(solution)/shard_map/all_to_all | solution.py:368
  41.4 0.0 copy-start
  41.4 1.3 copy-done
  42.8 17.5 %shard_map.94 = (bf16[1024,1152]{1,0:T(8,128)(2,1)}, f32[1]{0:T(128)}, bf16[1024,1024]{1,0:T(8,128)(2,1)}) custom-call(f32[2]{0:T(128)} %fusion.6.coef_ref, s32[1]{0:T(128)} %copy.10.dim_ref, bf16[1024,1024]{1,0:T(8,128)(2,1)} %bitcast.24, bf16[1,2,1024,1024]{3,2,1,0:T(8,128)(2,1)} %left_hbm.1, bf16[1,2,1024,1024]{3,2,1,0:T(8,128)(2,1)} %right_hbm.1), custom_call_target="tpu_custom_call" | custom-call | tf_op jit(solution)/shard_map/pallas_call | solution.py:355
  60.2 37.8 %all_to_all.25 = bf16[32,32,1152]{2,1,0:T(8,128)(2,1)S(1)} all-to-all(bf16[32,32,1152]{2,1,0:T(8,128)(2,1)} %bitcast.27), channel_id=1, replica_groups=mesh['sector'=4,'ops_0'=4,'ops_1'=4,'ops_2'=2] {'ops_0','ops_1','ops_2'}, dimensions={0} | all-to-all | bytes 4718592 | tf_op jit(solution)/shard_map/all_to_all | solution.py:378
  98.0 0.6 convert_element_type.33
  98.6 0.0 copy-start.2
  98.6 0.0 copy-start.3
  98.6 0.6 slice_reduce_fusion.1
  99.3 0.2 slice_reduce_fusion
  100.9 0.0 copy-done.2
  100.9 0.0 copy-done.3
  100.9 0.1 fusion.2
  101.0 0.1 broadcast_in_dim.52
  101.1 20.8 %all_to_all.26 = bf16[32,32,512]{2,1,0:T(8,128)(2,1)} all-to-all(bf16[32,32,512]{2,1,0:T(8,128)(2,1)S(1)} %broadcast_in_dim.52), channel_id=1, replica_groups=mesh['sector'=4,'ops_0'=4,'ops_1'=4,'ops_2'=2] {'ops_0','ops_1','ops_2'}, dimensions={0} | all-to-all | bytes 2097152 | tf_op jit(solution)/shard_map/all_to_all | solution.py:368
  121.9 1.1 broadcast_in_dim.51
  123.0 4.7 %all-to-all-start.2 = ((bf16[32,32,512]{2,1,0:T(8,128)(2,1)}), bf16[32,32,512]{2,1,0:T(8,128)(2,1)S(1)}, u32[]{:S(2)}, u32[]{:S(2)}) async-start(bf16[32,32,512]{2,1,0:T(8,128)(2,1)} %broadcast_in_dim.51), calls=%async_computation.2 | async-start | bytes 2097152 | tf_op jit(solution)/shard_map/all_to_all | solution.py:368
  127.8 0.7 pad_add_fusion.place_ref
  128.4 23.6 %shard_map.95 = (bf16[1024,512]{1,0:T(8,128)(2,1)}, bf16[1024,512]{1,0:T(8,128)(2,1)}, bf16[512,512]{1,0:T(8,128)(2,1)}, bf16[512,512]{1,0:T(8,128)(2,1)}, bf16[512,512]{1,0:T(8,128)(2,1)}, /*index=5*/f32[512,128]{1,0:T(8,128)}) custom-call(bf16[1024,512]{1,0:T(8,128)(2,1)} %bitcast.22), custom_call_target="tpu_custom_call" | custom-call | tf_op jit(solution)/shard_map/pallas_call | solution.py:273
  152.1 0.0 all-to-all-done.2
  152.1 0.0 copy-start.1
  152.1 1.0 copy-done.1
  153.1 35.8 %shard_map.96 = (bf16[32,1024]{1,0:T(8,128)(2,1)}, bf16[1024,512]{1,0:T(8,128)(2,1)}, bf16[1024,512]{1,0:T(8,128)(2,1)}) custom-call(s32[2]{0:T(128)} %pad_add_fusion.place_ref, bf16[1024,512]{1,0:T(8,128)(2,1)} %bitcast.26, bf16[1024,512]{1,0:T(8,128)(2,1)} %bitcast.23, f32[512,128]{1,0:T(8,128)} %get-tuple-element.17.refs_2_, ...), custom_call_target="tpu_custom_call" | custom-call | tf_op jit(solution)/shard_map/pallas_call | solution.py:285
  188.9 2.1 collective-permute-start
  191.0 2.5 %collective-permute-done = bf16[1024,512]{1,0:T(8,128)(2,1)S(1)} collective-permute-done((bf16[1024,512]{1,0:T(8,128)(2,1)}, bf16[1024,512]{1,0:T(8,128)(2,1)S(1)}, u32[]{:S(2)}, u32[]{:S(2)}) %collective-permute-start) | collective-permute-done | bytes 1048608 | tf_op jit(solution)/shard_map/ppermute | solution.py:406
  193.5 1.5 add_convert_fusion
  195.0 23.9 %all_to_all.27 = bf16[32,32,512]{2,1,0:T(8,128)(2,1)S(1)} all-to-all(bf16[32,32,512]{2,1,0:T(8,128)(2,1)S(1)} %bitcast.25), channel_id=1, replica_groups=mesh['sector'=4,'ops_0'=4,'ops_1'=4,'ops_2'=2] {'ops_0','ops_1','ops_2'}, dimensions={0} | all-to-all | bytes 2097152 | tf_op jit(solution)/shard_map/all_to_all | solution.py:378
  218.9 0.2 reduce_sum.42
  219.1 4.8 %collective-permute-start.3 = (bf16[32,512]{1,0:T(8,128)(2,1)S(1)}, bf16[32,512]{1,0:T(8,128)(2,1)S(1)}, u32[]{:S(2)}, u32[]{:S(2)}) collective-permute-start(bf16[32,512]{1,0:T(8,128)(2,1)S(1)} %reduce_sum.42), channel_id=1, source_target_pairs={{0,96},{32,64},{64,32},{96,0},{1,97},{33,65},{65,33},{97,1},{2,98}... | collective-permute-start | bytes 98312 | tf_op jit(solution)/shard_map/ppermute | solution.py:406
  223.8 0.0 collective-permute-start.2
  223.8 0.3 collective-permute-start.1
  224.2 1.8 collective-permute-done.3
  226.0 0.0 collective-permute-done.2
  226.0 2.1 collective-permute-done.1
  228.1 0.7 pad_maximum_fusion
  (4 shorter events, 0.0 us)
Async XLA Ops:
  3.9 9.9 %copy-start.4 = (f32[16]{0:T(128)S(1)}, f32[16]{0:T(128)}, u32[]{:S(2)}) copy-start(f32[16]{0:T(128)} %param.13) | copy-start | bytes 196
  3.9 9.9 %copy-start.5 = (s32[1,2]{1,0:T(1,128)S(1)}, s32[1,2]{1,0:T(1,128)}, u32[]{:S(2)}) copy-start(s32[1,2]{1,0:T(1,128)} %param.12) | copy-start | bytes 28
  3.9 37.6 %all-to-all-start = ((bf16[32,32,1024]{2,1,0:T(8,128)(2,1)}), bf16[32,32,1024]{2,1,0:T(8,128)(2,1)S(1)}, u32[]{:S(2)}, u32[]{:S(2)}) async-start(bf16[32,32,1024]{2,1,0:T(8,128)(2,1)} %broadcast_in_dim.50), calls=%async_computation | async-start | bytes 4194304 | tf_op jit(solution)/shard_map/all_to_all | solution.py:368
  41.4 1.3 copy-start
  98.6 2.2 copy-start.2
  98.6 2.2 copy-start.3
  123.0 29.1 %all-to-all-start.2 = ((bf16[32,32,512]{2,1,0:T(8,128)(2,1)}), bf16[32,32,512]{2,1,0:T(8,128)(2,1)S(1)}, u32[]{:S(2)}, u32[]{:S(2)}) async-start(bf16[32,32,512]{2,1,0:T(8,128)(2,1)} %broadcast_in_dim.51), calls=%async_computation.2 | async-start | bytes 2097152 | tf_op jit(solution)/shard_map/all_to_all | solution.py:368
  152.1 1.0 copy-start.1
  188.9 4.6 %collective-permute-start = (bf16[1024,512]{1,0:T(8,128)(2,1)}, bf16[1024,512]{1,0:T(8,128)(2,1)S(1)}, u32[]{:S(2)}, u32[]{:S(2)}) collective-permute-start(bf16[1024,512]{1,0:T(8,128)(2,1)} %get-tuple-element.26), channel_id=1, source_target_pairs={{0,32},{32,0},{64,96},{96,64},{1,33},{33,1},{65,97},{97,65},{2,34}... | collective-permute-start | bytes 3145736 | tf_op jit(solution)/shard_map/ppermute | solution.py:406
  219.1 7.0 %collective-permute-start.3 = (bf16[32,512]{1,0:T(8,128)(2,1)S(1)}, bf16[32,512]{1,0:T(8,128)(2,1)S(1)}, u32[]{:S(2)}, u32[]{:S(2)}) collective-permute-start(bf16[32,512]{1,0:T(8,128)(2,1)S(1)} %reduce_sum.42), channel_id=1, source_target_pairs={{0,96},{32,64},{64,32},{96,0},{1,97},{33,65},{65,33},{97,1},{2,98}... | collective-permute-start | bytes 98312 | tf_op jit(solution)/shard_map/ppermute | solution.py:406
  223.8 2.2 collective-permute-start.2
  223.8 4.3 %collective-permute-start.1 = (bf16[32,512]{1,0:T(8,128)(2,1)S(1)}, bf16[32,512]{1,0:T(8,128)(2,1)S(1)}, u32[]{:S(2)}, u32[]{:S(2)}) collective-permute-start(bf16[32,512]{1,0:T(8,128)(2,1)S(1)} %reduce_sum.42), channel_id=1, source_target_pairs={{0,64},{32,96},{64,0},{96,32},{1,65},{33,97},{65,1},{97,33},{2,66}... | collective-permute-start | bytes 98312 | tf_op jit(solution)/shard_map/ppermute | solution.py:406
